TPU v7x, 128 devices: a whole 4x4x4 slice. The times are simulated.
128 devices in a mesh: blk: 16 (over y_hi, x, core), hid: 8 (over y_lo, z).
Axes of the slice: x: 4, y: 4 (y_hi: 2, y_lo: 2; y = y_hi * 2 + y_lo), z: 4, core: 2. Of those that a mesh axis runs over, the one named last changes fastest.
Arguments:
- hyp_emb: bfloat16 [256, 1024], P('blk'), may hold values from -6 to 6
- ref_emb: bfloat16 [256, 1024], P('blk'), may hold values from -6 to 6
- hyp_part: bfloat16 [256, 3072], P('blk', 'hid'), may hold values from -4 to 4
- ref_part: bfloat16 [256, 3072], P('blk', 'hid'), may hold values from -4 to 4
- pair_weight: bfloat16 [2048, 3072], P(None, 'hid'), may hold values from -0.125 to 0.125
- out_weight: bfloat16 [3072, 1024], P('hid'), may hold values from -0.21875 to 0.21875
- out_bias: float32 [1024], P('hid'), may hold values from -4 to 4
- score_weight: float32 [1024], P('hid'), may hold values from -0.04 to 0.04
Outputs:
- scores: float32 [256, 256], P('blk')
- utilities: float32 [256], P('blk')
All inputs are finite; a program needn't handle non-finite values.
Results may differ from a plain program's by a relative error of at most 0.013.
Values may be sent and summed in bfloat16 or wider, within the bound.
A program may use at most 64 MiB of HBM per device.

v0:
```python
import jax
import jax.numpy as jnp
from jax import lax
from jax.sharding import PartitionSpec as P


def shifted(block, axis, distance):
    devices = range(lax.axis_size(axis))
    route = [((i - distance) % len(devices), i) for i in devices]
    return lax.ppermute(block, axis, route)


def body(hyp_emb, ref_emb, hyp_part, ref_part, pair_weight, out_weight, out_bias, score_weight):
    blocks = lax.axis_size("blk")
    mine = lax.axis_index("blk")
    hyp_rows = hyp_emb.shape[0]
    ref_rows = ref_emb.shape[0]
    pair_rows = hyp_rows * ref_rows
    left = hyp_emb.astype(jnp.float32)[:, None, :]
    hyp_terms = hyp_part.astype(jnp.float32)[:, None, :]

    def tile(panel_emb, panel_part):
        right = panel_emb.astype(jnp.float32)[None, :, :]
        prod = (left * right).astype(jnp.bfloat16).reshape(pair_rows, -1)
        diff = jnp.abs(left - right).astype(jnp.bfloat16).reshape(pair_rows, -1)
        feats = jnp.concatenate([prod, diff], axis=1)
        inner = jnp.dot(feats, pair_weight, preferred_element_type=jnp.float32).reshape(
            hyp_rows, ref_rows, -1
        )
        inner = inner + hyp_terms + panel_part.astype(jnp.float32)[None, :, :]
        first = jnp.tanh(inner).astype(jnp.bfloat16).reshape(pair_rows, -1)
        summed = lax.psum_scatter(
            lax.dot_general(
                out_weight, first, (((0,), (1,)), ((), ())), preferred_element_type=jnp.float32
            ).astype(jnp.bfloat16),
            "hid",
            scatter_dimension=0,
            tiled=True,
        ).astype(jnp.float32)
        second = jnp.tanh(summed + out_bias[:, None])
        partial_score = jnp.dot(score_weight, second, precision=lax.Precision.HIGHEST)
        partial_score = partial_score.reshape(hyp_rows, ref_rows)
        partial_score = lax.psum(partial_score, "hid")
        return partial_score

    def place(total, piece, owner):
        column = owner * ref_rows
        return lax.dynamic_update_slice(total, piece, (jnp.int32(0), column))

    start_total = jnp.zeros((hyp_rows, ref_rows * blocks), jnp.float32)
    total = place(start_total, tile(ref_emb, ref_part), mine)

    def turn(step, carry):
        running, panel_emb, panel_part = carry
        panel_emb, panel_part = shifted((panel_emb, panel_part), "blk", 1)
        owner = jnp.mod(mine - step, blocks)
        running = place(running, tile(panel_emb, panel_part), owner)
        return (running, panel_emb, panel_part)

    total, unused_emb, unused_part = lax.fori_loop(1, blocks, turn, (total, ref_emb, ref_part))
    utilities = jnp.mean(total, axis=1)
    return (total, utilities)


def solution(mesh):
    in_specs = (
        P("blk", None),
        P("blk", None),
        P("blk", "hid"),
        P("blk", "hid"),
        P(None, "hid"),
        P("hid", None),
        P("hid"),
        P("hid"),
    )
    out_specs = (P("blk", None), P("blk"))
    return jax.shard_map(body, mesh=mesh, in_specs=in_specs, out_specs=out_specs, check_vma=False)
```

profile of v0, /device:TPU:0, one launch (start us, length us, event | category | flops | bytes accessed | tf_op | source)
XLA Modules:
  0.0 1026.6 jit_solution(13716058523299641573)
XLA Ops:
  14.9 40.5 %reduce-scatter.9.cloned.1.call-done = bf16[128,256]{1,0:T(8,128)(2,1)} async-done(((bf16[1024,256]{1,0:T(8,128)(2,1)}), bf16[128,256]{1,0:T(8,128)(2,1)}) %reduce-scatter.9.cloned.1.call-update) | async-done | bytes 65552
  56.8 17.0 %psum.21 = f32[16,16]{1,0:T(8,128)S(1)} all-reduce(f32[16,16]{1,0:T(8,128)S(1)} %reshape.89), channel_id=1, replica_groups=mesh['blk'=16,'hid'=8] {'hid'}, use_global_device_ids=true, to_apply=%region_1.0 | all-reduce | flops 256 | bytes 2048 | tf_op jit(solution)/shard_map/psum | solution.py:43
  74.1 945.3 %while.19 = (s32[]{:T(128)}, f32[16,256]{1,0:T(8,128)S(1)}, bf16[16,1024]{1,0:T(8,128)(2,1)S(1)}, bf16[16,384]{1,0:T(8,128)(2,1)S(1)}, f32[16,1,1024]{2,1,0:T(1,...) while((s32[]{:T(128)}, f32[16,256]{1,0:T(8,128)S(1)}, ...), condition=%wide.region_5.6_spmd, body=%wide.region_2.5_spmd.sunk | while | flops 608426240 | bytes 9949624 | solution.py:60
  83.8 34.6 %reduce-scatter.11.cloned.1.call-done = bf16[128,256]{1,0:T(8,128)(2,1)} async-done(((bf16[1024,256]{1,0:T(8,128)(2,1)}), bf16[128,256]{1,0:T(8,128)(2,1)}) %reduce-scatter.11.cloned.1.call-update) | async-done | bytes 65552 | tf_op jit(solution)/shard_map/while
  119.7 17.0 %psum.23 = f32[16,16]{1,0:T(8,128)S(1)} all-reduce(f32[16,16]{1,0:T(8,128)S(1)} %reshape.99), channel_id=1, replica_groups=mesh['blk'=16,'hid'=8] {'hid'}, use_global_device_ids=true, to_apply=%region_4.4 | all-reduce | flops 256 | bytes 2048 | tf_op jit(solution)/shard_map/while/body/eval_jaxpr/psum | solution.py:43
  146.7 34.8 %reduce-scatter.11.cloned.1.call-done = bf16[128,256]{1,0:T(8,128)(2,1)} async-done(((bf16[1024,256]{1,0:T(8,128)(2,1)}), bf16[128,256]{1,0:T(8,128)(2,1)}) %reduce-scatter.11.cloned.1.call-update) | async-done | bytes 65552 | tf_op jit(solution)/shard_map/while
  182.8 17.0 %psum.23 = f32[16,16]{1,0:T(8,128)S(1)} all-reduce(f32[16,16]{1,0:T(8,128)S(1)} %reshape.99), channel_id=1, replica_groups=mesh['blk'=16,'hid'=8] {'hid'}, use_global_device_ids=true, to_apply=%region_4.4 | all-reduce | flops 256 | bytes 2048 | tf_op jit(solution)/shard_map/while/body/eval_jaxpr/psum | solution.py:43
  209.8 34.7 %reduce-scatter.11.cloned.1.call-done = bf16[128,256]{1,0:T(8,128)(2,1)} async-done(((bf16[1024,256]{1,0:T(8,128)(2,1)}), bf16[128,256]{1,0:T(8,128)(2,1)}) %reduce-scatter.11.cloned.1.call-update) | async-done | bytes 65552 | tf_op jit(solution)/shard_map/while
  245.7 17.0 %psum.23 = f32[16,16]{1,0:T(8,128)S(1)} all-reduce(f32[16,16]{1,0:T(8,128)S(1)} %reshape.99), channel_id=1, replica_groups=mesh['blk'=16,'hid'=8] {'hid'}, use_global_device_ids=true, to_apply=%region_4.4 | all-reduce | flops 256 | bytes 2048 | tf_op jit(solution)/shard_map/while/body/eval_jaxpr/psum | solution.py:43
  272.7 34.8 %reduce-scatter.11.cloned.1.call-done = bf16[128,256]{1,0:T(8,128)(2,1)} async-done(((bf16[1024,256]{1,0:T(8,128)(2,1)}), bf16[128,256]{1,0:T(8,128)(2,1)}) %reduce-scatter.11.cloned.1.call-update) | async-done | bytes 65552 | tf_op jit(solution)/shard_map/while
  308.8 16.9 %psum.23 = f32[16,16]{1,0:T(8,128)S(1)} all-reduce(f32[16,16]{1,0:T(8,128)S(1)} %reshape.99), channel_id=1, replica_groups=mesh['blk'=16,'hid'=8] {'hid'}, use_global_device_ids=true, to_apply=%region_4.4 | all-reduce | flops 256 | bytes 2048 | tf_op jit(solution)/shard_map/while/body/eval_jaxpr/psum | solution.py:43
  335.8 34.9 %reduce-scatter.11.cloned.1.call-done = bf16[128,256]{1,0:T(8,128)(2,1)} async-done(((bf16[1024,256]{1,0:T(8,128)(2,1)}), bf16[128,256]{1,0:T(8,128)(2,1)}) %reduce-scatter.11.cloned.1.call-update) | async-done | bytes 65552 | tf_op jit(solution)/shard_map/while
  371.9 16.9 %psum.23 = f32[16,16]{1,0:T(8,128)S(1)} all-reduce(f32[16,16]{1,0:T(8,128)S(1)} %reshape.99), channel_id=1, replica_groups=mesh['blk'=16,'hid'=8] {'hid'}, use_global_device_ids=true, to_apply=%region_4.4 | all-reduce | flops 256 | bytes 2048 | tf_op jit(solution)/shard_map/while/body/eval_jaxpr/psum | solution.py:43
  398.8 34.9 %reduce-scatter.11.cloned.1.call-done = bf16[128,256]{1,0:T(8,128)(2,1)} async-done(((bf16[1024,256]{1,0:T(8,128)(2,1)}), bf16[128,256]{1,0:T(8,128)(2,1)}) %reduce-scatter.11.cloned.1.call-update) | async-done | bytes 65552 | tf_op jit(solution)/shard_map/while
  435.0 16.9 %psum.23 = f32[16,16]{1,0:T(8,128)S(1)} all-reduce(f32[16,16]{1,0:T(8,128)S(1)} %reshape.99), channel_id=1, replica_groups=mesh['blk'=16,'hid'=8] {'hid'}, use_global_device_ids=true, to_apply=%region_4.4 | all-reduce | flops 256 | bytes 2048 | tf_op jit(solution)/shard_map/while/body/eval_jaxpr/psum | solution.py:43
  462.0 34.9 %reduce-scatter.11.cloned.1.call-done = bf16[128,256]{1,0:T(8,128)(2,1)} async-done(((bf16[1024,256]{1,0:T(8,128)(2,1)}), bf16[128,256]{1,0:T(8,128)(2,1)}) %reduce-scatter.11.cloned.1.call-update) | async-done | bytes 65552 | tf_op jit(solution)/shard_map/while
  498.1 16.9 %psum.23 = f32[16,16]{1,0:T(8,128)S(1)} all-reduce(f32[16,16]{1,0:T(8,128)S(1)} %reshape.99), channel_id=1, replica_groups=mesh['blk'=16,'hid'=8] {'hid'}, use_global_device_ids=true, to_apply=%region_4.4 | all-reduce | flops 256 | bytes 2048 | tf_op jit(solution)/shard_map/while/body/eval_jaxpr/psum | solution.py:43
  525.1 34.8 %reduce-scatter.11.cloned.1.call-done = bf16[128,256]{1,0:T(8,128)(2,1)} async-done(((bf16[1024,256]{1,0:T(8,128)(2,1)}), bf16[128,256]{1,0:T(8,128)(2,1)}) %reduce-scatter.11.cloned.1.call-update) | async-done | bytes 65552 | tf_op jit(solution)/shard_map/while
  561.1 17.0 %psum.23 = f32[16,16]{1,0:T(8,128)S(1)} all-reduce(f32[16,16]{1,0:T(8,128)S(1)} %reshape.99), channel_id=1, replica_groups=mesh['blk'=16,'hid'=8] {'hid'}, use_global_device_ids=true, to_apply=%region_4.4 | all-reduce | flops 256 | bytes 2048 | tf_op jit(solution)/shard_map/while/body/eval_jaxpr/psum | solution.py:43
  588.1 34.8 %reduce-scatter.11.cloned.1.call-done = bf16[128,256]{1,0:T(8,128)(2,1)} async-done(((bf16[1024,256]{1,0:T(8,128)(2,1)}), bf16[128,256]{1,0:T(8,128)(2,1)}) %reduce-scatter.11.cloned.1.call-update) | async-done | bytes 65552 | tf_op jit(solution)/shard_map/while
  624.2 17.0 %psum.23 = f32[16,16]{1,0:T(8,128)S(1)} all-reduce(f32[16,16]{1,0:T(8,128)S(1)} %reshape.99), channel_id=1, replica_groups=mesh['blk'=16,'hid'=8] {'hid'}, use_global_device_ids=true, to_apply=%region_4.4 | all-reduce | flops 256 | bytes 2048 | tf_op jit(solution)/shard_map/while/body/eval_jaxpr/psum | solution.py:43
  651.3 34.6 %reduce-scatter.11.cloned.1.call-done = bf16[128,256]{1,0:T(8,128)(2,1)} async-done(((bf16[1024,256]{1,0:T(8,128)(2,1)}), bf16[128,256]{1,0:T(8,128)(2,1)}) %reduce-scatter.11.cloned.1.call-update) | async-done | bytes 65552 | tf_op jit(solution)/shard_map/while
  687.1 17.0 %psum.23 = f32[16,16]{1,0:T(8,128)S(1)} all-reduce(f32[16,16]{1,0:T(8,128)S(1)} %reshape.99), channel_id=1, replica_groups=mesh['blk'=16,'hid'=8] {'hid'}, use_global_device_ids=true, to_apply=%region_4.4 | all-reduce | flops 256 | bytes 2048 | tf_op jit(solution)/shard_map/while/body/eval_jaxpr/psum | solution.py:43
  714.2 34.6 %reduce-scatter.11.cloned.1.call-done = bf16[128,256]{1,0:T(8,128)(2,1)} async-done(((bf16[1024,256]{1,0:T(8,128)(2,1)}), bf16[128,256]{1,0:T(8,128)(2,1)}) %reduce-scatter.11.cloned.1.call-update) | async-done | bytes 65552 | tf_op jit(solution)/shard_map/while
  750.0 17.0 %psum.23 = f32[16,16]{1,0:T(8,128)S(1)} all-reduce(f32[16,16]{1,0:T(8,128)S(1)} %reshape.99), channel_id=1, replica_groups=mesh['blk'=16,'hid'=8] {'hid'}, use_global_device_ids=true, to_apply=%region_4.4 | all-reduce | flops 256 | bytes 2048 | tf_op jit(solution)/shard_map/while/body/eval_jaxpr/psum | solution.py:43
  777.1 34.7 %reduce-scatter.11.cloned.1.call-done = bf16[128,256]{1,0:T(8,128)(2,1)} async-done(((bf16[1024,256]{1,0:T(8,128)(2,1)}), bf16[128,256]{1,0:T(8,128)(2,1)}) %reduce-scatter.11.cloned.1.call-update) | async-done | bytes 65552 | tf_op jit(solution)/shard_map/while
  813.1 17.0 %psum.23 = f32[16,16]{1,0:T(8,128)S(1)} all-reduce(f32[16,16]{1,0:T(8,128)S(1)} %reshape.99), channel_id=1, replica_groups=mesh['blk'=16,'hid'=8] {'hid'}, use_global_device_ids=true, to_apply=%region_4.4 | all-reduce | flops 256 | bytes 2048 | tf_op jit(solution)/shard_map/while/body/eval_jaxpr/psum | solution.py:43
  840.1 34.7 %reduce-scatter.11.cloned.1.call-done = bf16[128,256]{1,0:T(8,128)(2,1)} async-done(((bf16[1024,256]{1,0:T(8,128)(2,1)}), bf16[128,256]{1,0:T(8,128)(2,1)}) %reduce-scatter.11.cloned.1.call-update) | async-done | bytes 65552 | tf_op jit(solution)/shard_map/while
  903.1 34.7 %reduce-scatter.11.cloned.1.call-done = bf16[128,256]{1,0:T(8,128)(2,1)} async-done(((bf16[1024,256]{1,0:T(8,128)(2,1)}), bf16[128,256]{1,0:T(8,128)(2,1)}) %reduce-scatter.11.cloned.1.call-update) | async-done | bytes 65552 | tf_op jit(solution)/shard_map/while
  939.0 17.0 %psum.23 = f32[16,16]{1,0:T(8,128)S(1)} all-reduce(f32[16,16]{1,0:T(8,128)S(1)} %reshape.99), channel_id=1, replica_groups=mesh['blk'=16,'hid'=8] {'hid'}, use_global_device_ids=true, to_apply=%region_4.4 | all-reduce | flops 256 | bytes 2048 | tf_op jit(solution)/shard_map/while/body/eval_jaxpr/psum | solution.py:43
  966.1 34.7 %reduce-scatter.11.cloned.1.call-done = bf16[128,256]{1,0:T(8,128)(2,1)} async-done(((bf16[1024,256]{1,0:T(8,128)(2,1)}), bf16[128,256]{1,0:T(8,128)(2,1)}) %reduce-scatter.11.cloned.1.call-update) | async-done | bytes 65552 | tf_op jit(solution)/shard_map/while
  1002.0 17.0 %psum.23 = f32[16,16]{1,0:T(8,128)S(1)} all-reduce(f32[16,16]{1,0:T(8,128)S(1)} %reshape.99), channel_id=1, replica_groups=mesh['blk'=16,'hid'=8] {'hid'}, use_global_device_ids=true, to_apply=%region_4.4 | all-reduce | flops 256 | bytes 2048 | tf_op jit(solution)/shard_map/while/body/eval_jaxpr/psum | solution.py:43
  (350 shorter events, 194.3 us)
Async XLA Ops:
  7.2 48.3 %reduce-scatter.9.cloned.1.call-start = ((), (), s32[]{:S(2)}) async-start(), calls=%async_computation.2 | async-start | bytes 589824
  74.1 44.3 %reduce-scatter.11.cloned.1.call-start = ((), (), s32[]{:S(2)}) async-start(), calls=%async_computation.3 | async-start | bytes 589824 | tf_op jit(solution)/shard_map/while
  74.1 7.2 collective-permute-start.1
  74.2 7.1 collective-permute-start
  137.0 44.5 %reduce-scatter.11.cloned.1.call-start = ((), (), s32[]{:S(2)}) async-start(), calls=%async_computation.3 | async-start | bytes 589824 | tf_op jit(solution)/shard_map/while
  137.0 7.2 collective-permute-start.1
  200.1 44.4 %reduce-scatter.11.cloned.1.call-start = ((), (), s32[]{:S(2)}) async-start(), calls=%async_computation.3 | async-start | bytes 589824 | tf_op jit(solution)/shard_map/while
  200.1 7.2 collective-permute-start.1
  263.0 44.5 %reduce-scatter.11.cloned.1.call-start = ((), (), s32[]{:S(2)}) async-start(), calls=%async_computation.3 | async-start | bytes 589824 | tf_op jit(solution)/shard_map/while
  263.1 7.2 collective-permute-start.1
  326.1 44.6 %reduce-scatter.11.cloned.1.call-start = ((), (), s32[]{:S(2)}) async-start(), calls=%async_computation.3 | async-start | bytes 589824 | tf_op jit(solution)/shard_map/while
  326.1 7.2 collective-permute-start.1
  389.1 44.6 %reduce-scatter.11.cloned.1.call-start = ((), (), s32[]{:S(2)}) async-start(), calls=%async_computation.3 | async-start | bytes 589824 | tf_op jit(solution)/shard_map/while
  389.2 7.2 collective-permute-start.1
  452.3 44.6 %reduce-scatter.11.cloned.1.call-start = ((), (), s32[]{:S(2)}) async-start(), calls=%async_computation.3 | async-start | bytes 589824 | tf_op jit(solution)/shard_map/while
  452.3 7.2 collective-permute-start.1
  515.4 44.5 %reduce-scatter.11.cloned.1.call-start = ((), (), s32[]{:S(2)}) async-start(), calls=%async_computation.3 | async-start | bytes 589824 | tf_op jit(solution)/shard_map/while
  515.4 7.2 collective-permute-start.1
  578.4 44.5 %reduce-scatter.11.cloned.1.call-start = ((), (), s32[]{:S(2)}) async-start(), calls=%async_computation.3 | async-start | bytes 589824 | tf_op jit(solution)/shard_map/while
  578.5 7.2 collective-permute-start.1
  641.5 44.3 %reduce-scatter.11.cloned.1.call-start = ((), (), s32[]{:S(2)}) async-start(), calls=%async_computation.3 | async-start | bytes 589824 | tf_op jit(solution)/shard_map/while
  641.6 7.2 collective-permute-start.1
  704.5 44.3 %reduce-scatter.11.cloned.1.call-start = ((), (), s32[]{:S(2)}) async-start(), calls=%async_computation.3 | async-start | bytes 589824 | tf_op jit(solution)/shard_map/while
  704.5 7.2 collective-permute-start.1
  767.3 44.5 %reduce-scatter.11.cloned.1.call-start = ((), (), s32[]{:S(2)}) async-start(), calls=%async_computation.3 | async-start | bytes 589824 | tf_op jit(solution)/shard_map/while
  767.4 7.2 collective-permute-start.1
  830.4 44.4 %reduce-scatter.11.cloned.1.call-start = ((), (), s32[]{:S(2)}) async-start(), calls=%async_computation.3 | async-start | bytes 589824 | tf_op jit(solution)/shard_map/while
  830.5 7.2 collective-permute-start.1
  893.4 44.4 %reduce-scatter.11.cloned.1.call-start = ((), (), s32[]{:S(2)}) async-start(), calls=%async_computation.3 | async-start | bytes 589824 | tf_op jit(solution)/shard_map/while
  893.4 7.2 collective-permute-start.1
  956.4 44.4 %reduce-scatter.11.cloned.1.call-start = ((), (), s32[]{:S(2)}) async-start(), calls=%async_computation.3 | async-start | bytes 589824 | tf_op jit(solution)/shard_map/while
  956.4 7.2 collective-permute-start.1
  (21 other events, 253.8 us)
Sparse Core Ops, SparseCore 0:
  15.0 40.4 reduce-scatter.8
  83.9 34.4 reduce-scatter.10
  146.8 34.7 reduce-scatter.10
  209.8 34.5 reduce-scatter.10
  272.8 34.7 reduce-scatter.10
  335.8 34.7 reduce-scatter.10
  398.9 34.8 reduce-scatter.10
  462.0 34.7 reduce-scatter.10
  525.1 34.7 reduce-scatter.10
  588.2 34.7 reduce-scatter.10
  651.3 34.4 reduce-scatter.10
  714.2 34.4 reduce-scatter.10
  777.1 34.6 reduce-scatter.10
  840.2 34.5 reduce-scatter.10
  903.1 34.5 reduce-scatter.10
  966.2 34.5 reduce-scatter.10
where the time goes:
time: 1030 us
  waiting for transfers between devices  644 us (63%)
  blocking collectives  272 us (26%)
  local copies, waits for them, and re-layouts  41.9 us (4%)
  starting transfers between devices  25.2 us (2%)
  matrix products  23.2 us (2%)
  between operations  13.9 us (1%)
    while x30, waiting for transfers between devices  521 us
    psum x16, blocking collectives, tile(): partial_score = lax.psum(partial_score, 'hid')  272 us
    ppermute x30, waiting for transfers between devices, shifted(): return lax.ppermute(block, axis, route)  82.1 us
    unnamed x2, waiting for transfers between devices  40.6 us
    while x90, local copies, waits for them, and re-layouts  29.5 us
    ppermute x30, starting transfers between devices, shifted(): return lax.ppermute(block, axis, route)  24.7 us
  transfers between devices with their start and end apart: 46, of which 31 were waited for; matrix products, arithmetic and copies ran while one was open for 0% of the time, Pallas kernels for 0%

commit v1 on v0

v1 whole, which is shorter than its diff:
```python
import functools

import jax
import jax.numpy as jnp
from jax import lax
from jax.experimental import pallas as pl
from jax.experimental.pallas import tpu as pltpu
from jax.sharding import PartitionSpec as P

MESH = pl.DeviceIdType.MESH
BF16 = jnp.bfloat16
F32 = jnp.float32

STEPS1 = 8
STEPS2 = 4
STEPS = STEPS1 + STEPS2
K1 = 2048 // STEPS1
Q1 = K1 // 4
C2 = 1024 // STEPS2
U = 384
AHEAD = 3


def mod(a, n):
    return lax.rem(a, jnp.int32(n))


def half(a):
    return lax.div(a, jnp.int32(2))


def device(x, y, z, c):
    return ((half(y) * 4 + x) * 2 + c, mod(y, 2) * 4 + z)


def slot_of(rel):
    return rel + half(rel) * (5 - 2 * rel)


SLOT_AT = {0: 0, 1: 2, 2: 3, 3: 1}


def kernel(
    hyp_emb, ref_emb, hyp_part, ref_part, w1_in, w2_in, bias_in, score_in,
    scores_out, util_out,
    w1, w2, hyp, ref, hp, rp, bs, feats, acc, first, part_send, part_recv, part_mine, sc, sm,
    hypf, hpf, rpf, sacc,
    z_recv, x_recv, d_recv, z_send, x_send, d_send,
    small_recv, hp_send, rp_send, ref_send, bs_send, loc, pr_recv, pr_send, sc_send,
):
    blk = lax.axis_index("blk")
    hid = lax.axis_index("hid")
    c = mod(blk, 2)
    x = mod(half(blk), 4)
    y_hi = lax.div(blk, jnp.int32(8))
    y_lo = lax.div(hid, jnp.int32(4))
    y = y_hi * 2 + y_lo
    z = mod(hid, 4)

    def zz(d):
        return mod(z + d, 4)

    def yy(d):
        return mod(y + d, 4)

    def xx(d):
        return mod(x + d, 4)

    sibling = device(x, y, z, 1 - c)
    z_up, z_down = device(x, y, zz(1), c), device(x, y, zz(3), c)
    x_up, x_down = device(xx(1), y, z, c), device(xx(3), y, z, c)

    ref_j = mod(c + y_lo, 2)
    ref_y = mod(y + 2 * c * (1 - y_lo), 4)
    ref_self = jnp.logical_and(ref_y == y, x == z)

    barrier = pltpu.get_barrier_semaphore()

    def greet(target):
        pl.semaphore_signal(barrier, inc=1, device_id=target, device_id_type=MESH)

    for dy in range(4):
        for dz in range(4):
            if dy or dz:
                greet(device(x, yy(dy), zz(dz), c))
    greet(sibling)
    greet(x_up)
    greet(x_down)
    for j in range(2):
        e = yy(4 - j)
        src_y = half(e) * 2 + y_lo
        src_c = mod(e, 2)
        for dz in range(4):
            is_me = (
                jnp.logical_and(jnp.logical_and(src_y == y, src_c == c), x == z) if dz == 0 else None
            )
            target = device(z, src_y, zz(dz), src_c)
            if is_me is None:
                greet(target)
            else:
                pl.when(jnp.logical_not(is_me))(functools.partial(greet, target))
    pl.semaphore_wait(barrier, 15 + 3 + 8 - jnp.where(ref_self, 1, 0))

    def remote(src, dst, send, recv, target):
        pltpu.make_async_remote_copy(
            src_ref=src, dst_ref=dst, send_sem=send, recv_sem=recv, device_id=target, device_id_type=MESH
        ).start()

    def local(src, dst, sem):
        pltpu.make_async_copy(src, dst, sem).start()

    def done(region, sem):
        pltpu.make_async_copy(region, region, sem).wait()

    quarter = mod(x, 2) * 2 + c
    quarter_x = (1 - mod(x, 2)) * 2 + c

    def region(t, quarter_, slots):
        lo, n = slots
        if t < STEPS1:
            rows = pl.ds(pl.multiple_of(t * K1 + quarter_ * Q1, Q1), Q1)
            return w1.at[rows, pl.ds(lo * U, n * U)]
        rows = pl.ds(pl.multiple_of(quarter_ * 96, 96), 96)
        return w2.at[pl.ds(lo, n), rows, pl.ds((t - STEPS1) * C2, C2)]

    def own_piece(t):
        if t < STEPS1:
            rows = pl.ds(pl.multiple_of(t * K1 + quarter * Q1, Q1), Q1)
            return w1_in.at[rows, :]
        rows = pl.ds(pl.multiple_of(quarter * 96, 96), 96)
        return w2_in.at[:, rows, pl.ds((t - STEPS1) * C2, C2)]

    def send_own(t):
        remote(own_piece(t), region(t, quarter, (1, 1)), z_send.at[0, t], z_recv.at[0, t], z_down)
        remote(own_piece(t), region(t, quarter, (2, 1)), z_send.at[1, t], z_recv.at[1, t], z_up)

    local(hyp_emb, hyp.at[0], small_recv.at[0])
    remote(hyp_emb, hyp.at[1], loc.at[3], small_recv.at[0], device(x, yy(2), z, c))

    def send_refs():
        for k in range(8):
            dx, dc = k // 2, k % 2
            target = device(xx(dx), ref_y, z, mod(c + dc, 2))
            if k == 0:
                pl.when(ref_self)(lambda: local(ref_emb, ref.at[ref_j], small_recv.at[1]))
                pl.when(jnp.logical_not(ref_self))(
                    lambda: remote(ref_emb, ref.at[ref_j], ref_send.at[k], small_recv.at[1], target)
                )
            else:
                remote(ref_emb, ref.at[ref_j], ref_send.at[k], small_recv.at[1], target)

    pl.when(x == z)(send_refs)
    send_own(0)
    local(w1_in, w1.at[:, pl.ds(0, U)], loc.at[0])
    local(w2_in, w2.at[pl.ds(0, 1)], loc.at[1])
    local(hyp_part, hp.at[0, 0], small_recv.at[2])
    for d in range(1, 4):
        remote(hyp_part, hp.at[0, SLOT_AT[d]], hp_send.at[d], small_recv.at[2], device(x, y, zz(d), c))
    for d in range(4):
        remote(hyp_part, hp.at[1, SLOT_AT[d]], hp_send.at[4 + d], small_recv.at[2], device(x, yy(2), zz(d), c))
    ref_slot = slot_of(mod(z - x + 4, 4))
    for k in range(8):
        dx, dc = k // 2, k % 2
        target = device(xx(dx), ref_y, x, mod(c + dc, 2))
        there = rp.at[ref_j, ref_slot]
        if k == 0:
            pl.when(ref_self)(lambda: local(ref_part, there, small_recv.at[3]))
            pl.when(jnp.logical_not(ref_self))(
                lambda: remote(ref_part, there, rp_send.at[k], small_recv.at[3], target)
            )
        else:
            remote(ref_part, there, rp_send.at[k], small_recv.at[3], target)
    for t in range(1, AHEAD):
        send_own(t)
    bs[hid] = jnp.concatenate([bias_in[...], score_in[...], jnp.zeros((6, 128), F32)], axis=0)
    for d in range(1, 8):
        remote(bs.at[hid], bs.at[hid], bs_send.at[d], small_recv.at[4], (blk, mod(hid + d, 8)))

    def forward_z(t):
        done(region(t, quarter, (1, 1)), z_recv.at[0, t])
        done(region(t, quarter, (2, 1)), z_recv.at[1, t])
        if t % 2 == 0:
            remote(region(t, quarter, (1, 1)), region(t, quarter, (3, 1)), z_send.at[2, t], z_recv.at[2, t], z_down)
        else:
            remote(region(t, quarter, (2, 1)), region(t, quarter, (3, 1)), z_send.at[2, t], z_recv.at[2, t], z_up)
        two = region(t, quarter, (1, 2))
        remote(two, two, x_send.at[0, t], x_recv.at[0, t], x_up if t % 2 == 0 else x_down)
        if t + AHEAD < STEPS:
            send_own(t + AHEAD)
        remote(two, two, d_send.at[0, t], d_recv.at[0, t], sibling)

    def forward_z3(t):
        one = region(t, quarter, (3, 1))
        done(one, z_recv.at[2, t])
        remote(one, one, x_send.at[1, t], x_recv.at[1, t], x_up if t % 2 == 0 else x_down)
        remote(one, one, d_send.at[1, t], d_recv.at[1, t], sibling)

    def forward_x(t):
        two = region(t, quarter_x, (1, 2))
        done(two, x_recv.at[0, t])
        remote(two, two, d_send.at[2, t], d_recv.at[2, t], sibling)

    def forward_x3(t):
        one = region(t, quarter_x, (3, 1))
        done(one, x_recv.at[1, t])
        remote(one, one, d_send.at[3, t], d_recv.at[3, t], sibling)

    def arrived(t):
        other, other_x = quarter + 1 - 2 * c, quarter_x + 1 - 2 * c
        done(region(t, other, (1, 2)), d_recv.at[0, t])
        done(region(t, other, (3, 1)), d_recv.at[1, t])
        done(region(t, other_x, (1, 2)), d_recv.at[2, t])
        done(region(t, other_x, (3, 1)), d_recv.at[3, t])

    def drain(t):
        done(own_piece(t), z_send.at[0, t])
        done(own_piece(t), z_send.at[1, t])
        one, two = region(t, quarter, (3, 1)), region(t, quarter, (1, 2))
        done(one, z_send.at[2, t])
        done(two, x_send.at[0, t])
        done(one, x_send.at[1, t])
        done(two, d_send.at[0, t])
        done(one, d_send.at[1, t])
        done(two, d_send.at[2, t])
        done(one, d_send.at[3, t])

    def make_feats():
        done(hyp, small_recv.at[0])
        done(ref, small_recv.at[1])
        hypf[...] = hyp[...].astype(F32).reshape(32, 1024)
        right = [ref[j].astype(F32) for j in range(2)]

        def one(h, carry):
            left = hypf[pl.ds(h, 1), :]
            for j in range(2):
                rows = pl.ds(pl.multiple_of(j * 512 + h * 16, 16), 16)
                feats[rows, pl.ds(0, 1024)] = (left * right[j]).astype(BF16)
                feats[rows, pl.ds(1024, 1024)] = jnp.abs(left - right[j]).astype(BF16)
            return carry

        lax.fori_loop(0, 32, one, 0)

    def multiply(k, depth, begin):
        def block(i, carry):
            rows = pl.ds(pl.multiple_of(i * 256, 256), 256)
            left = feats[rows, pl.ds(k, depth)]
            for n in range(3):
                columns = pl.ds(n * 512, 512)
                value = jnp.dot(left, w1[pl.ds(k, depth), columns], preferred_element_type=F32)
                if not begin:
                    value = acc[rows, columns] + value
                acc[rows, columns] = value
            return carry

        lax.fori_loop(0, 4, block, 0)

    def make_parts():
        done(hp, small_recv.at[2])
        done(rp, small_recv.at[3])
        for s in range(2):
            for g in range(4):
                hpf[s, :, pl.ds(g * U, U)] = hp[s, g].astype(F32)
                rpf[s, :, pl.ds(g * U, U)] = rp[s, g].astype(F32)

    mine = mod(y_hi + y_lo, 2)

    def finish_first(k, depth):
        def block(i, carry):
            edge = mod(i, 2)
            slot = jnp.where(i < 2, 1 - mine, mine)
            base = pl.multiple_of(edge * 512 + slot * 256, 256)
            rows = pl.ds(base, 256)
            left = feats[rows, pl.ds(k, depth)]
            for n in range(3):
                columns = pl.ds(n * 512, 512)
                acc[rows, columns] += jnp.dot(left, w1[pl.ds(k, depth), columns], preferred_element_type=F32)

            def one(h, carry):
                here = pl.ds(pl.multiple_of(base + h * 16, 16), 16)
                there = pl.ds(pl.multiple_of(i * 256 + h * 16, 16), 16)
                value = acc[here, :] + hpf[slot, pl.ds(h, 1), :] + rpf[edge]
                first[there, :] = jnp.tanh(value).astype(BF16)
                return carry

            lax.fori_loop(0, 16, one, 0)
            return carry

        lax.fori_loop(0, 4, block, 0)

    def second_weights(n):
        return w2[:, :, pl.ds(n * C2, C2)].reshape(4 * U, C2)

    def theirs(n):
        columns = pl.ds(n * C2, C2)
        for j in range(2):
            value = jnp.dot(first[pl.ds(j * 256, 256), :], second_weights(n), preferred_element_type=F32)
            part_send[j, :, columns] = value.astype(BF16)
            remote(
                part_send.at[j, :, columns], part_recv.at[1 - j, :, columns], pr_send.at[j, n], pr_recv.at[1 - j, n],
                device(x, yy(1) if j == 0 else yy(3), z, c),
            )

    def ours(n):
        for j in range(2):
            part_mine[j, :, pl.ds(n * C2, C2)] = jnp.dot(
                first[pl.ds(512 + j * 256, 256), :], second_weights(n), preferred_element_type=F32
            )

    def finish_second(n):
        columns = pl.ds(n * C2, C2)
        for j in range(2):
            done(part_recv.at[j, :, columns], pr_recv.at[j, n])
            total = jnp.zeros((256, 128), F32) if n == 0 else sacc[j]
            for k in range(C2 // 128):
                g = n * (C2 // 128) + k
                lanes = pl.ds(g * 128, 128)
                value = part_mine[j, :, lanes] + part_recv[j, :, lanes].astype(F32)
                total += jnp.tanh(value + bs[g, 0:1, :]) * bs[g, 1:2, :]
            sacc[j] = total

    for t in range(STEPS + 3):
        if t < STEPS:
            forward_z(t)
        if 0 <= t - 1 < STEPS:
            forward_z3(t - 1)
            forward_x(t - 1)
        if 0 <= t - 2 < STEPS:
            forward_x3(t - 2)
        if t == 1:
            make_feats()
        if t == 2:
            make_parts()
            done(w1_in, loc.at[0])
            done(w2_in, loc.at[1])
        a = t - 3
        if 0 <= a:
            arrived(a)
        if a in (1, 3, 5):
            multiply((a - 1) * K1, 2 * K1, a == 1)
        if a == 7:
            finish_first(6 * K1, 2 * K1)
        if a >= STEPS1:
            theirs(a - STEPS1)
            ours(a - STEPS1)
    done(bs.at[pl.ds(0, 7)], small_recv.at[4])
    for n in range(STEPS2):
        finish_second(n)

    lane = lax.broadcasted_iota(jnp.int32, (256, 128), 1)
    row = lax.broadcasted_iota(jnp.int32, (256, 128), 0)
    sums = [jnp.zeros((16, 128), F32), jnp.zeros((16, 128), F32)]
    for j in range(2):
        e = yy(4 - j)
        place = z * 32 + mod(e, 2) * 16
        value = jnp.sum(sacc[j], axis=1, keepdims=True)
        value = jnp.where(lane - place == jnp.bitwise_and(row, 15), value, 0.0)
        value = jnp.sum(value.reshape(16, 16, 128), axis=1)
        for k in range(2):
            sums[k] += jnp.where(half(e) == k, value, 0.0)
    sm[:, pl.ds(0, 128)] = sums[0]
    sm[:, pl.ds(128, 128)] = sums[1]

    sc_row = y_hi * 4 + z
    sc_self = mod(y, 2) == y_hi
    for d in range(8):
        target = (mod(y, 2) * 8 + mod(blk, 8), mod(hid + d, 8))
        if d == 0:
            pl.when(sc_self)(lambda: local(sm, sc.at[sc_row], small_recv.at[5]))
            pl.when(jnp.logical_not(sc_self))(
                lambda: remote(sm, sc.at[sc_row], sc_send.at[d], small_recv.at[5], target)
            )
        else:
            remote(sm, sc.at[sc_row], sc_send.at[d], small_recv.at[5], target)

    for t in range(STEPS):
        drain(t)
    done(hyp_emb, loc.at[3])
    for d in range(1, 8):
        done(hyp_part, hp_send.at[d])
        done(bs.at[0], bs_send.at[d])
    for k in range(8):
        if k == 0:
            pl.when(jnp.logical_and(x == z, jnp.logical_not(ref_self)))(lambda: done(ref_emb, ref_send.at[0]))
            pl.when(jnp.logical_not(ref_self))(lambda: done(ref_part, rp_send.at[0]))
        else:
            pl.when(x == z)(lambda: done(ref_emb, ref_send.at[k]))
            done(ref_part, rp_send.at[k])
    for j in range(2):
        for n in range(STEPS2):
            done(part_send.at[j, :, pl.ds(n * C2, C2)], pr_send.at[j, n])

    done(sc, small_recv.at[5])
    total = sc[0]
    for k in range(1, 8):
        total += sc[k]
    scores_out[...] = total
    mean = jnp.sum(total, axis=1, keepdims=True) * (1.0 / 256.0)
    lane = lax.broadcasted_iota(jnp.int32, (16, 128), 1)
    row = lax.broadcasted_iota(jnp.int32, (16, 128), 0)
    spread = jnp.sum(jnp.where(lane == row, mean, 0.0), axis=0, keepdims=True)
    util_out[...] = spread[:, :16]

    for d in range(8):
        if d == 0:
            pl.when(jnp.logical_not(sc_self))(lambda: done(sm, sc_send.at[0]))
        else:
            done(sm, sc_send.at[d])


def body(hyp_emb, ref_emb, hyp_part, ref_part, pair_weight, out_weight, out_bias, score_weight):
    any_space = pl.BlockSpec(memory_space=pl.ANY)
    vmem = pl.BlockSpec(memory_space=pltpu.VMEM)
    dma = pltpu.SemaphoreType.DMA
    scores, utilities = pl.pallas_call(
        kernel,
        out_shape=(jax.ShapeDtypeStruct((16, 256), F32), jax.ShapeDtypeStruct((1, 16), F32)),
        in_specs=[any_space] * 6 + [vmem] * 2,
        out_specs=(vmem, vmem),
        scratch_shapes=[
            pltpu.VMEM((2048, 4 * U), BF16),
            pltpu.VMEM((4, U, 1024), BF16),
            pltpu.VMEM((2, 16, 1024), BF16),
            pltpu.VMEM((2, 16, 1024), BF16),
            pltpu.VMEM((2, 4, 16, U), BF16),
            pltpu.VMEM((2, 4, 16, U), BF16),
            pltpu.VMEM((8, 8, 128), F32),
            pltpu.VMEM((1024, 2048), BF16),
            pltpu.VMEM((1024, 4 * U), F32),
            pltpu.VMEM((1024, 4 * U), BF16),
            pltpu.VMEM((2, 256, 1024), BF16),
            pltpu.VMEM((2, 256, 1024), BF16),
            pltpu.VMEM((2, 256, 1024), F32),
            pltpu.VMEM((8, 16, 256), F32),
            pltpu.VMEM((16, 256), F32),
            pltpu.VMEM((32, 1024), F32),
            pltpu.VMEM((2, 16, 4 * U), F32),
            pltpu.VMEM((2, 16, 4 * U), F32),
            pltpu.VMEM((2, 256, 128), F32),
            dma((3, STEPS)), dma((2, STEPS)), dma((4, STEPS)),
            dma((3, STEPS)), dma((2, STEPS)), dma((4, STEPS)),
            dma((6,)), dma((8,)), dma((8,)), dma((8,)), dma((8,)), dma((4,)),
            dma((2, STEPS2)), dma((2, STEPS2)), dma((8,)),
        ],
        compiler_params=pltpu.CompilerParams(
            collective_id=0, has_side_effects=True, vmem_limit_bytes=50 * 2**20
        ),
        cost_estimate=pl.CostEstimate(flops=9_663_676_416, bytes_accessed=3_000_000, transcendentals=2_097_152),
        name="mbr_scores",
    )(
        hyp_emb, ref_emb, hyp_part, ref_part, pair_weight, out_weight.reshape(1, U, 1024),
        out_bias.reshape(1, 128), score_weight.reshape(1, 128),
    )
    return scores, utilities.reshape(16)


def solution(mesh):
    in_specs = (
        P("blk", None),
        P("blk", None),
        P("blk", "hid"),
        P("blk", "hid"),
        P(None, "hid"),
        P("hid", None),
        P("hid"),
        P("hid"),
    )
    out_specs = (P("blk", None), P("blk"))
    return jax.shard_map(body, mesh=mesh, in_specs=in_specs, out_specs=out_specs, check_vma=False)
```

time: 1030 us -> 80.4 us (0.08)
  waiting for transfers between devices: 644 us -> 0 us
  blocking collectives: 272 us -> 0 us
  Pallas kernels: 0 us -> 71.4 us
  local copies, waits for them, and re-layouts: 41.9 us -> 7.89 us
  starting transfers between devices: 25.2 us -> 0 us
  matrix products: 23.2 us -> 0 us
  between operations: 13.9 us -> 0.66 us
    while x30 -> x0, waiting for transfers between devices: 521 us -> none
    psum x16 -> x0, blocking collectives: 272 us -> none  [tile(): partial_score = lax.psum(partial_score, 'hid')]
    ppermute x30 -> x0, waiting for transfers between devices: 82.1 us -> none  [shifted(): return lax.ppermute(block, axis, route)]
    pallas_call x0 -> x1, Pallas kernels: none -> 71.4 us  [body(): pl.pallas_call(kernel, out_shape=(jax.ShapeDtypeStruct((16, 256), F32), j...]
    unnamed x2 -> x0, waiting for transfers between devices: 40.6 us -> none
    while x90 -> x0, local copies, waits for them, and re-layouts: 29.5 us -> none
    ppermute x30 -> x0, starting transfers between devices: 24.7 us -> none  [shifted(): return lax.ppermute(block, axis, route)]
    dot_general x47 -> x0, matrix products: 23.2 us -> none  [the longest x15 11 us: tile(): jnp.dot(feats, pair_weight, preferred_element_type=jnp.float32)]
  transfers between devices with their start and end apart: 46 -> 0, of which waited for: 31 -> 0; matrix products, arithmetic and copies ran while one was open for 0% -> 0% of each run, Pallas kernels for 0% -> 0%
where the time goes in v1:
time: 80.4 us; the launch traced here: 80 us
  Pallas kernels  71.4 us (89%)
  local copies, waits for them, and re-layouts  7.89 us (10%)
    pallas_call x1, Pallas kernels, body(): pl.pallas_call(kernel, out_shape=(jax.ShapeDtypeStruct((16, 256), F32), j...  71.4 us
    unnamed x18, local copies, waits for them, and re-layouts  7.89 us

profile of v1, /device:TPU:0, one launch (start us, length us, event | category | flops | bytes accessed | tf_op | source)
XLA Modules:
  0.0 80.0 jit_solution(7852334092027096225)
XLA Ops:
  0.6 0.0 copy-start
  0.6 1.4 %copy-done = bf16[2048,384]{1,0:T(8,128)(2,1)S(1)} copy-done((bf16[2048,384]{1,0:T(8,128)(2,1)S(1)}, bf16[2048,384]{1,0:T(8,128)(2,1)}, u32[]{:S(2)}) %copy-start) | copy-done | bytes 1572888
  2.0 0.0 copy-start.1
  2.0 1.1 %copy-done.1 = bf16[384,1024]{1,0:T(8,128)(2,1)S(1)} copy-done((bf16[384,1024]{1,0:T(8,128)(2,1)S(1)}, bf16[384,1024]{1,0:T(8,128)(2,1)}, u32[]{:S(2)}) %copy-start.1) | copy-done | bytes 786456
  3.2 0.0 copy-start.2
  3.2 0.8 copy-done.2
  3.9 0.0 copy-start.3
  3.9 0.8 copy-done.3
  4.7 0.0 copy-start.4
  4.7 0.7 copy-done.4
  5.4 0.0 copy-start.5
  5.4 0.7 copy-done.5
  6.1 0.0 copy-start.6
  6.1 0.7 copy-done.6
  6.8 0.0 copy-start.7
  6.8 0.7 copy-done.7
  7.4 71.4 %mbr_scores.1 = (f32[16,256]{1,0:T(8,128)S(1)}, f32[1,16]{1,0:T(1,128)S(1)}) custom-call(bf16[16,1024]{1,0:T(8,128)(2,1)S(1)} %copy-done.2, bf16[16,1024]{1,0:T(8,128)(2,1)S(1)} %copy-done.3, bf16[16,384]{1,0:T(8,128)(2,1)S(1)} %copy-done.4, bf16[16,384]{1,0:T(8,128)(2,1)S(1)} %copy-done.5, bf16[2048,384]{1,0:T(8,128)(2,1)S(1)} %copy-done, ...), custom_call_target="tpu_custom_call" | custom-call | flops 9663676416 | bytes 3000000 | tf_op jit(solution)/shard_map/mbr_scores/pallas_call | solution.py:414
  78.9 0.6 copy.12
  79.5 0.5 copy.13
Async XLA Ops:
  0.6 1.4 %copy-start = (bf16[2048,384]{1,0:T(8,128)(2,1)S(1)}, bf16[2048,384]{1,0:T(8,128)(2,1)}, u32[]{:S(2)}) copy-start(bf16[2048,384]{1,0:T(8,128)(2,1)} %w1_in.1) | copy-start | bytes 4718596
  2.0 1.1 %copy-start.1 = (bf16[384,1024]{1,0:T(8,128)(2,1)S(1)}, bf16[384,1024]{1,0:T(8,128)(2,1)}, u32[]{:S(2)}) copy-start(bf16[384,1024]{1,0:T(8,128)(2,1)} %param.13) | copy-start | bytes 2359300
  3.2 0.8 copy-start.2
  3.9 0.8 copy-start.3
  4.7 0.7 copy-start.4
  5.4 0.7 copy-start.5
  6.1 0.7 copy-start.6
  6.8 0.7 copy-start.7

commit v2 on v1

v2 whole, which is shorter than its diff:
```python
import functools

import jax
import jax.numpy as jnp
from jax import lax
from jax.experimental import pallas as pl
from jax.experimental.pallas import tpu as pltpu
from jax.sharding import PartitionSpec as P

MESH = pl.DeviceIdType.MESH
BF16 = jnp.bfloat16
F32 = jnp.float32

STEPS1 = 8
STEPS2 = 4
STEPS = STEPS1 + STEPS2
K1 = 2048 // STEPS1
Q1 = K1 // 4
C2 = 1024 // STEPS2
U = 384
AHEAD = 2
LZ3, LX, LX3, L12, L3 = 2, 2, 4, 3, 5


def mod(a, n):
    return lax.rem(a, jnp.int32(n))


def half(a):
    return lax.div(a, jnp.int32(2))


def device(x, y, z, c):
    return ((half(y) * 4 + x) * 2 + c, mod(y, 2) * 4 + z)


def slot_of(rel):
    return rel + half(rel) * (5 - 2 * rel)


SLOT_AT = {0: 0, 1: 2, 2: 3, 3: 1}


def kernel(
    hyp_emb, ref_emb, hyp_part, ref_part, w1_in, w2_in, bias_in, score_in,
    scores_out, util_out,
    w1, w2, hyp, ref, hp, rp, bs, my_bs, feats, acc, first, part_send, part_recv, part_mine, sc, sm,
    hypf, hpf, rpf, sacc,
    z_recv, z3_recv, x_recv, x3_recv, d_recv, d3_recv, w_send, small_recv, small_send, loc, pr_recv,
):
    blk = lax.axis_index("blk")
    hid = lax.axis_index("hid")
    c = mod(blk, 2)
    x = mod(half(blk), 4)
    y_hi = lax.div(blk, jnp.int32(8))
    y_lo = lax.div(hid, jnp.int32(4))
    y = y_hi * 2 + y_lo
    z = mod(hid, 4)

    def zz(d):
        return mod(z + d, 4)

    def yy(d):
        return mod(y + d, 4)

    def xx(d):
        return mod(x + d, 4)

    sibling = device(x, y, z, 1 - c)
    z_up, z_down = device(x, y, zz(1), c), device(x, y, zz(3), c)
    x_up, x_down = device(xx(1), y, z, c), device(xx(3), y, z, c)

    ref_j = mod(c + y_lo, 2)
    ref_y = mod(y + 2 * c * (1 - y_lo), 4)
    ref_self = jnp.logical_and(ref_y == y, x == z)

    barrier = pltpu.get_barrier_semaphore()

    def greet(target):
        pl.semaphore_signal(barrier, inc=1, device_id=target, device_id_type=MESH)

    for dy in range(4):
        for dz in range(4):
            if dy or dz:
                greet(device(x, yy(dy), zz(dz), c))
    greet(sibling)
    greet(x_up)
    greet(x_down)
    for j in range(2):
        e = yy(4 - j)
        src_y = half(e) * 2 + y_lo
        src_c = mod(e, 2)
        for dz in range(4):
            is_me = (
                jnp.logical_and(jnp.logical_and(src_y == y, src_c == c), x == z) if dz == 0 else None
            )
            target = device(z, src_y, zz(dz), src_c)
            if is_me is None:
                greet(target)
            else:
                pl.when(jnp.logical_not(is_me))(functools.partial(greet, target))
    pl.semaphore_wait(barrier, 15 + 3 + 8 - jnp.where(ref_self, 1, 0))

    def remote(src, dst, send, recv, target):
        pltpu.make_async_remote_copy(
            src_ref=src, dst_ref=dst, send_sem=send, recv_sem=recv, device_id=target, device_id_type=MESH
        ).start()

    def local(src, dst, sem):
        pltpu.make_async_copy(src, dst, sem).start()

    def done(region, sem):
        pltpu.make_async_copy(region, region, sem).wait()

    quarter = mod(x, 2) * 2 + c
    quarter_x = (1 - mod(x, 2)) * 2 + c

    def region(t, quarter_, slots, part=None):
        lo, n = slots
        size = Q1 if t < STEPS1 else 96
        first_row = quarter_ * size
        if part is not None:
            size //= 2
            first_row += part * size
        if t < STEPS1:
            rows = pl.ds(pl.multiple_of(t * K1 + first_row, size), size)
            return w1.at[rows, pl.ds(lo * U, n * U)]
        rows = pl.ds(pl.multiple_of(first_row, size), size)
        return w2.at[pl.ds(lo, n), rows, pl.ds((t - STEPS1) * C2, C2)]

    def own_piece(t):
        if t < STEPS1:
            rows = pl.ds(pl.multiple_of(t * K1 + quarter * Q1, Q1), Q1)
            return w1_in.at[rows, :]
        rows = pl.ds(pl.multiple_of(quarter * 96, 96), 96)
        return w2_in.at[:, rows, pl.ds((t - STEPS1) * C2, C2)]

    def send(src, dst, recv, target, t):
        remote(src, dst, w_send.at[0 if t < STEPS1 else 1], recv, target)

    def send_own(t):
        send(own_piece(t), region(t, quarter, (1, 1)), z_recv.at[t], z_down, t)
        send(own_piece(t), region(t, quarter, (2, 1)), z_recv.at[t], z_up, t)

    local(hyp_emb, hyp.at[0], small_recv.at[0])
    remote(hyp_emb, hyp.at[1], small_send.at[0], small_recv.at[0], device(x, yy(2), z, c))

    def send_refs():
        for k in range(8):
            dx, dc = k // 2, k % 2
            target = device(xx(dx), ref_y, z, mod(c + dc, 2))
            if k == 0:
                pl.when(ref_self)(lambda: local(ref_emb, ref.at[ref_j], small_recv.at[1]))
                pl.when(jnp.logical_not(ref_self))(
                    lambda: remote(ref_emb, ref.at[ref_j], small_send.at[1], small_recv.at[1], target)
                )
            else:
                remote(ref_emb, ref.at[ref_j], small_send.at[1], small_recv.at[1], target)

    for t in range(AHEAD):
        send_own(t)
    pl.when(x == z)(send_refs)
    local(w1_in, w1.at[:, pl.ds(0, U)], loc.at[0])
    local(w2_in, w2.at[pl.ds(0, 1)], loc.at[1])
    local(bias_in, my_bs.at[0], loc.at[2])
    local(score_in, my_bs.at[1], loc.at[3])
    local(hyp_part, hp.at[0], small_recv.at[2])
    for d in range(1, 4):
        remote(hyp_part, hp.at[SLOT_AT[d]], small_send.at[2], small_recv.at[2], device(x, y, zz(d), c))
    for d in range(4):
        remote(hyp_part, hp.at[4 + SLOT_AT[d]], small_send.at[2], small_recv.at[2], device(x, yy(2), zz(d), c))
    ref_slot = slot_of(mod(z - x + 4, 4))
    for k in range(8):
        dx, dc = k // 2, k % 2
        target = device(xx(dx), ref_y, x, mod(c + dc, 2))
        there = rp.at[ref_j * 4 + ref_slot]
        if k == 0:
            pl.when(ref_self)(lambda: local(ref_part, there, small_recv.at[3]))
            pl.when(jnp.logical_not(ref_self))(
                lambda: remote(ref_part, there, small_send.at[3], small_recv.at[3], target)
            )
        else:
            remote(ref_part, there, small_send.at[3], small_recv.at[3], target)

    def send_bias():
        done(bias_in, loc.at[2])
        done(score_in, loc.at[3])
        local(my_bs, bs.at[hid], small_recv.at[4])
        for d in range(1, 8):
            remote(my_bs, bs.at[hid], small_send.at[4], small_recv.at[4], (blk, mod(hid + d, 8)))

    def forward_z(t):
        two = region(t, quarter, (1, 2))
        done(two, z_recv.at[t])
        send(region(t, quarter, (1, 1), 0), region(t, quarter, (3, 1), 0), z3_recv.at[t], z_down, t)
        send(region(t, quarter, (2, 1), 1), region(t, quarter, (3, 1), 1), z3_recv.at[t], z_up, t)
        for part, target in ((0, x_up), (1, x_down)):
            piece = region(t, quarter, (1, 2), part)
            send(piece, piece, x_recv.at[t], target, t)
        if t + AHEAD < STEPS:
            send_own(t + AHEAD)
        send(two, two, d_recv.at[t], sibling, t)

    def forward_z3(t):
        one = region(t, quarter, (3, 1))
        done(one, z3_recv.at[t])
        for part, target in ((0, x_up), (1, x_down)):
            piece = region(t, quarter, (3, 1), part)
            send(piece, piece, x3_recv.at[t], target, t)
        send(one, one, d3_recv.at[t], sibling, t)

    def forward_x(t):
        two = region(t, quarter_x, (1, 2))
        done(two, x_recv.at[t])
        send(two, two, d_recv.at[t], sibling, t)

    def forward_x3(t):
        one = region(t, quarter_x, (3, 1))
        done(one, x3_recv.at[t])
        send(one, one, d3_recv.at[t], sibling, t)

    def arrived(t):
        if t < STEPS1:
            done(w1.at[pl.ds(0, 2 * Q1), pl.ds(0, 2 * U)], d_recv.at[t])
        else:
            done(w2.at[pl.ds(0, 2), pl.ds(0, 192), pl.ds(0, C2)], d_recv.at[t])

    def arrived3(t):
        if t < STEPS1:
            done(w1.at[pl.ds(0, 2 * Q1), pl.ds(0, U)], d3_recv.at[t])
        else:
            done(w2.at[pl.ds(0, 1), pl.ds(0, 192), pl.ds(0, C2)], d3_recv.at[t])

    def make_feats():
        done(hyp, small_recv.at[0])
        done(ref, small_recv.at[1])
        hypf[...] = hyp[...].astype(F32).reshape(32, 1024)
        right = [ref[j].astype(F32) for j in range(2)]

        def one(h, carry):
            left = hypf[pl.ds(h, 1), :]
            for j in range(2):
                rows = pl.ds(pl.multiple_of(j * 512 + h * 16, 16), 16)
                feats[rows, pl.ds(0, 1024)] = (left * right[j]).astype(BF16)
                feats[rows, pl.ds(1024, 1024)] = jnp.abs(left - right[j]).astype(BF16)
            return carry

        lax.fori_loop(0, 32, one, 0)

    mine = mod(y_hi + y_lo, 2)

    K = 2 * K1
    EARLY = pl.ds(0, 1024)
    LATE = pl.ds(1024, 512)

    def multiply(p, rows, columns):
        value = jnp.dot(feats[rows, pl.ds(p * K, K)], w1[pl.ds(p * K, K), columns], preferred_element_type=F32)
        if p:
            value = acc[rows, columns] + value
        acc[rows, columns] = value

    def block_rows(i):
        slot = 1 - mine if i < 2 else mine
        return slot, pl.multiple_of((i % 2) * 512 + slot * 256, 256)

    def activate(i, columns):
        slot, base = block_rows(i)

        def one(h, carry):
            here = pl.ds(pl.multiple_of(base + h * 16, 16), 16)
            there = pl.ds(pl.multiple_of(i * 256 + h * 16, 16), 16)
            value = acc[here, columns] + hpf[slot, pl.ds(h, 1), columns] + rpf[i % 2, :, columns]
            first[there, columns] = jnp.tanh(value).astype(BF16)
            return carry

        lax.fori_loop(0, 16, one, 0)

    def make_parts():
        done(hp, small_recv.at[2])
        done(rp, small_recv.at[3])
        for s in range(2):
            for g in range(4):
                hpf[s, :, pl.ds(g * U, U)] = hp[s * 4 + g].astype(F32)
                rpf[s, :, pl.ds(g * U, U)] = rp[s * 4 + g].astype(F32)

    def second_weights(n):
        return w2[:, :, pl.ds(n * C2, C2)].reshape(4 * U, C2)

    def theirs(n):
        columns = pl.ds(n * C2, C2)
        for j in range(2):
            value = jnp.dot(first[pl.ds(j * 256, 256), :], second_weights(n), preferred_element_type=F32)
            part_send[j, :, columns] = value.astype(BF16)
            remote(
                part_send.at[j, :, columns], part_recv.at[1 - j, :, columns], small_send.at[5], pr_recv.at[1 - j, n],
                device(x, yy(1) if j == 0 else yy(3), z, c),
            )

    def ours(n):
        for j in range(2):
            part_mine[j, :, pl.ds(n * C2, C2)] = jnp.dot(
                first[pl.ds(512 + j * 256, 256), :], second_weights(n), preferred_element_type=F32
            )

    def finish_second(n):
        columns = pl.ds(n * C2, C2)
        for j in range(2):
            done(part_recv.at[j, :, columns], pr_recv.at[j, n])
            total = jnp.zeros((256, 128), F32) if n == 0 else sacc[j]
            for k in range(C2 // 128):
                g = n * (C2 // 128) + k
                lanes = pl.ds(g * 128, 128)
                value = part_mine[j, :, lanes] + part_recv[j, :, lanes].astype(F32)
                total += jnp.tanh(value + bs[g, 0]) * bs[g, 1]
            sacc[j] = total

    for t in range(STEPS + L3):
        if t < STEPS:
            forward_z(t)
        if 0 <= t - LZ3 < STEPS:
            forward_z3(t - LZ3)
        if 0 <= t - LX < STEPS:
            forward_x(t - LX)
        if 0 <= t - LX3 < STEPS:
            forward_x3(t - LX3)
        if t == 0:
            send_bias()
        if t == 1:
            make_feats()
        if t == 2:
            make_parts()
            done(w1_in, loc.at[0])
            done(w2_in, loc.at[1])
        if 0 <= t - L12 < STEPS:
            arrived(t - L12)
        if 0 <= t - L3 < STEPS:
            arrived3(t - L3)
        a, b = t - L12 - 1, t - L3 - 1
        for i in range(4):
            rows = pl.ds(block_rows(i)[1], 256)
            if 0 <= a < STEPS1 and i // 2 == a % 2:
                multiply(a // 2, rows, EARLY)
                if a // 2 == 3:
                    activate(i, EARLY)
            if 0 <= b < STEPS1 - 2 and i // 2 == b % 2:
                multiply(b // 2, rows, LATE)
        if b == STEPS1 - 2:
            for i in range(4):
                multiply(3, pl.ds(block_rows(i)[1], 256), LATE)
                activate(i, LATE)
        n = t - L3 - STEPS1
        if n >= 0:
            theirs(n)
            ours(n)
    done(bs, small_recv.at[4])
    for n in range(STEPS2):
        finish_second(n)

    lane = lax.broadcasted_iota(jnp.int32, (256, 128), 1)
    row = lax.broadcasted_iota(jnp.int32, (256, 128), 0)
    value = jnp.zeros((16, 128), F32)
    for j in range(2):
        place = z * 32 + mod(yy(4 - j), 2) * 16
        total = jnp.sum(sacc[j], axis=1, keepdims=True)
        total = jnp.where(lane - place == jnp.bitwise_and(row, 15), total, 0.0)
        value += jnp.sum(total.reshape(16, 16, 128), axis=1)
    sm[...] = value

    sc_row = y_hi * 4 + z
    sc_self = mod(y, 2) == y_hi
    for d in range(8):
        target = (mod(y, 2) * 8 + mod(blk, 8), mod(hid + d, 8))
        if d == 0:
            pl.when(sc_self)(lambda: local(sm, sc.at[sc_row], small_recv.at[5]))
            pl.when(jnp.logical_not(sc_self))(
                lambda: remote(sm, sc.at[sc_row], small_send.at[6], small_recv.at[5], target)
            )
        else:
            remote(sm, sc.at[sc_row], small_send.at[6], small_recv.at[5], target)

    done(w1.at[pl.ds(0, 3 * 512), :], w_send.at[0])
    done(w2.at[pl.ds(0, 3)], w_send.at[1])
    done(hyp.at[0], small_send.at[0])
    done(hp.at[pl.ds(0, 7)], small_send.at[2])
    done(bs.at[pl.ds(0, 7)], small_send.at[4])
    done(part_send, small_send.at[5])

    def drain_refs():
        done(rp.at[pl.ds(0, 7)], small_send.at[3])
        done(feats.at[pl.ds(0, 112), pl.ds(0, 1024)], small_send.at[1])

    def drain_others():
        done(rp, small_send.at[3])
        pl.when(x == z)(lambda: done(feats.at[pl.ds(0, 128), pl.ds(0, 1024)], small_send.at[1]))

    pl.when(ref_self)(drain_refs)
    pl.when(jnp.logical_not(ref_self))(drain_others)

    done(sc, small_recv.at[5])
    halves = [sc[4 * k] + sc[4 * k + 1] + sc[4 * k + 2] + sc[4 * k + 3] for k in range(2)]
    lane = lax.broadcasted_iota(jnp.int32, (16, 128), 1)
    row = lax.broadcasted_iota(jnp.int32, (16, 128), 0)
    cross = jnp.bitwise_and(lane, 16) * (1 - y_hi) != 0
    halves = [jnp.where(cross, halves[1 - k], halves[k]) for k in range(2)]
    scores_out[:, pl.ds(0, 128)] = halves[0]
    scores_out[:, pl.ds(128, 128)] = halves[1]
    mean = jnp.sum(halves[0] + halves[1], axis=1, keepdims=True) * (1.0 / 256.0)
    util_out[...] = jnp.sum(jnp.where(lane == row, mean, 0.0), axis=0, keepdims=True)[:, :16]

    pl.when(sc_self)(lambda: done(sc.at[pl.ds(0, 7)], small_send.at[6]))
    pl.when(jnp.logical_not(sc_self))(lambda: done(sc, small_send.at[6]))


def body(hyp_emb, ref_emb, hyp_part, ref_part, pair_weight, out_weight, out_bias, score_weight):
    hbm = pl.BlockSpec(memory_space=pltpu.HBM)
    vmem = pl.BlockSpec(memory_space=pltpu.VMEM)
    dma = pltpu.SemaphoreType.DMA
    scores, utilities = pl.pallas_call(
        kernel,
        out_shape=(jax.ShapeDtypeStruct((16, 256), F32), jax.ShapeDtypeStruct((1, 16), F32)),
        in_specs=[hbm] * 8,
        out_specs=(vmem, vmem),
        scratch_shapes=[
            pltpu.VMEM((2048, 4 * U), BF16),
            pltpu.VMEM((4, U, 1024), BF16),
            pltpu.VMEM((2, 16, 1024), BF16),
            pltpu.VMEM((2, 16, 1024), BF16),
            pltpu.VMEM((8, 16, U), BF16),
            pltpu.VMEM((8, 16, U), BF16),
            pltpu.VMEM((8, 2, 1, 128), F32),
            pltpu.VMEM((2, 1, 128), F32),
            pltpu.VMEM((1024, 2048), BF16),
            pltpu.VMEM((1024, 4 * U), F32),
            pltpu.VMEM((1024, 4 * U), BF16),
            pltpu.VMEM((2, 256, 1024), BF16),
            pltpu.VMEM((2, 256, 1024), BF16),
            pltpu.VMEM((2, 256, 1024), F32),
            pltpu.VMEM((8, 16, 128), F32),
            pltpu.VMEM((16, 128), F32),
            pltpu.VMEM((32, 1024), F32),
            pltpu.VMEM((2, 16, 4 * U), F32),
            pltpu.VMEM((2, 16, 4 * U), F32),
            pltpu.VMEM((2, 256, 128), F32),
            dma((STEPS,)), dma((STEPS,)), dma((STEPS,)), dma((STEPS,)), dma((STEPS,)), dma((STEPS,)),
            dma((2,)), dma((6,)), dma((7,)), dma((4,)), dma((2, STEPS2)),
        ],
        compiler_params=pltpu.CompilerParams(
            collective_id=0, has_side_effects=True, vmem_limit_bytes=60 * 2**20
        ),
        cost_estimate=pl.CostEstimate(flops=9_663_676_416, bytes_accessed=3_000_000, transcendentals=2_097_152),
        name="mbr_scores",
    )(
        hyp_emb, ref_emb, hyp_part, ref_part, pair_weight, out_weight.reshape(1, U, 1024),
        out_bias.reshape(1, 128), score_weight.reshape(1, 128),
    )
    return scores, utilities.reshape(16)


def solution(mesh):
    in_specs = (
        P("blk", None),
        P("blk", None),
        P("blk", "hid"),
        P("blk", "hid"),
        P(None, "hid"),
        P("hid", None),
        P("hid"),
        P("hid"),
    )
    out_specs = (P("blk", None), P("blk"))
    return jax.shard_map(body, mesh=mesh, in_specs=in_specs, out_specs=out_specs, check_vma=False)
```

time: 80.4 us -> 64.5 us (0.80)
  Pallas kernels: 71.4 us -> 61.2 us
  local copies, waits for them, and re-layouts: 7.89 us -> 2.46 us
    pallas_call x1, Pallas kernels: 71.4 us -> 61.2 us  [body(): pl.pallas_call(kernel, out_shape=(jax.ShapeDtypeStruct((16, 256), F32), j...]
    unnamed x18 -> x2, local copies, waits for them, and re-layouts: 7.89 us -> 2.46 us
where the time goes in v2:
time: 64.5 us; the launch traced here: 64.3 us
  Pallas kernels  61.2 us (95%)
  local copies, waits for them, and re-layouts  2.46 us (4%)
    pallas_call x1, Pallas kernels, body(): pl.pallas_call(kernel, out_shape=(jax.ShapeDtypeStruct((16, 256), F32), j...  61.2 us
    unnamed x2, local copies, waits for them, and re-layouts  2.46 us

profile of v2, /device:TPU:0, one launch (start us, length us, event | category | flops | bytes accessed | tf_op | source)
XLA Modules:
  0.0 64.3 jit_solution(9475838074725553918)
XLA Ops:
  0.6 61.2 %mbr_scores.1 = (f32[16,256]{1,0:T(8,128)}, f32[1,16]{1,0:T(1,128)}) custom-call(bf16[16,1024]{1,0:T(8,128)(2,1)} %hyp_emb.1, bf16[16,1024]{1,0:T(8,128)(2,1)} %ref_emb.1, bf16[16,384]{1,0:T(8,128)(2,1)} %hyp_part.1, bf16[16,384]{1,0:T(8,128)(2,1)} %ref_part.1, bf16[2048,384]{1,0:T(8,128)(2,1)} %w1_in.1, bf16[1,384,1024]{2,1,0:T(8,128)(2,1)} %bitcast.4, ...), custom_call_target="tpu_custom_call" | custom-call | flops 9663676416 | bytes 3000000 | tf_op jit(solution)/shard_map/mbr_scores/pallas_call | solution.py:418
  61.8 1.3 %copy.12 = f32[16,256]{1,0:T(8,128)} copy(f32[16,256]{1,0:T(8,128)} %get-tuple-element.8) | data formatting | bytes 32768
  63.2 1.1 %copy.13 = f32[16]{0:T(128)} copy(f32[16]{0:T(128)} %bitcast.7) | data formatting | bytes 128

commit v3 on v2

--- a/solution.py
+++ b/solution.py
@@ -18,7 +18,7 @@
 Q1 = K1 // 4
 C2 = 1024 // STEPS2
 U = 384
-AHEAD = 2
+AHEAD = 3
 LZ3, LX, LX3, L12, L3 = 2, 2, 4, 3, 5
 
 
@@ -43,7 +43,7 @@
 
 def kernel(
     hyp_emb, ref_emb, hyp_part, ref_part, w1_in, w2_in, bias_in, score_in,
-    scores_out, util_out,
+    scores_out,
     w1, w2, hyp, ref, hp, rp, bs, my_bs, feats, acc, first, part_send, part_recv, part_mine, sc, sm,
     hypf, hpf, rpf, sacc,
     z_recv, z3_recv, x_recv, x3_recv, d_recv, d3_recv, w_send, small_recv, small_send, loc, pr_recv,
@@ -86,20 +86,15 @@
     greet(sibling)
     greet(x_up)
     greet(x_down)
-    for j in range(2):
-        e = yy(4 - j)
-        src_y = half(e) * 2 + y_lo
-        src_c = mod(e, 2)
-        for dz in range(4):
-            is_me = (
-                jnp.logical_and(jnp.logical_and(src_y == y, src_c == c), x == z) if dz == 0 else None
-            )
-            target = device(z, src_y, zz(dz), src_c)
-            if is_me is None:
-                greet(target)
-            else:
-                pl.when(jnp.logical_not(is_me))(functools.partial(greet, target))
-    pl.semaphore_wait(barrier, 15 + 3 + 8 - jnp.where(ref_self, 1, 0))
+    src_y = half(mod(y + 4 - ref_j, 4)) * 2 + y_lo
+    src_self = jnp.logical_and(src_y == y, x == z)
+    for dz in range(4):
+        source = device(z, src_y, zz(dz), c)
+        if dz == 0:
+            pl.when(jnp.logical_not(src_self))(functools.partial(greet, source))
+        else:
+            greet(source)
+    pl.semaphore_wait(barrier, 15 + 3 + 4 - jnp.where(ref_self, 1, 0))
 
     def remote(src, dst, send, recv, target):
         pltpu.make_async_remote_copy(
@@ -146,9 +141,8 @@
     remote(hyp_emb, hyp.at[1], small_send.at[0], small_recv.at[0], device(x, yy(2), z, c))
 
     def send_refs():
-        for k in range(8):
-            dx, dc = k // 2, k % 2
-            target = device(xx(dx), ref_y, z, mod(c + dc, 2))
+        for k in range(4):
+            target = device(xx(k), ref_y, z, c)
             if k == 0:
                 pl.when(ref_self)(lambda: local(ref_emb, ref.at[ref_j], small_recv.at[1]))
                 pl.when(jnp.logical_not(ref_self))(
@@ -170,10 +164,9 @@
     for d in range(4):
         remote(hyp_part, hp.at[4 + SLOT_AT[d]], small_send.at[2], small_recv.at[2], device(x, yy(2), zz(d), c))
     ref_slot = slot_of(mod(z - x + 4, 4))
-    for k in range(8):
-        dx, dc = k // 2, k % 2
-        target = device(xx(dx), ref_y, x, mod(c + dc, 2))
-        there = rp.at[ref_j * 4 + ref_slot]
+    for k in range(4):
+        target = device(xx(k), ref_y, x, c)
+        there = rp.at[ref_j, ref_slot]
         if k == 0:
             pl.when(ref_self)(lambda: local(ref_part, there, small_recv.at[3]))
             pl.when(jnp.logical_not(ref_self))(
@@ -181,6 +174,14 @@
             )
         else:
             remote(ref_part, there, small_send.at[3], small_recv.at[3], target)
+
+    def hand_refs():
+        done(ref.at[ref_j], small_recv.at[1])
+        remote(ref.at[ref_j], ref.at[ref_j], small_send.at[7], small_recv.at[6], sibling)
+
+    def hand_ref_parts():
+        done(rp.at[ref_j], small_recv.at[3])
+        remote(rp.at[ref_j], rp.at[ref_j], small_send.at[8], small_recv.at[7], sibling)
 
     def send_bias():
         done(bias_in, loc.at[2])
@@ -233,7 +234,7 @@
 
     def make_feats():
         done(hyp, small_recv.at[0])
-        done(ref, small_recv.at[1])
+        done(ref.at[1 - ref_j], small_recv.at[6])
         hypf[...] = hyp[...].astype(F32).reshape(32, 1024)
         right = [ref[j].astype(F32) for j in range(2)]
 
@@ -277,11 +278,11 @@
 
     def make_parts():
         done(hp, small_recv.at[2])
-        done(rp, small_recv.at[3])
+        done(rp.at[1 - ref_j], small_recv.at[7])
         for s in range(2):
             for g in range(4):
                 hpf[s, :, pl.ds(g * U, U)] = hp[s * 4 + g].astype(F32)
-                rpf[s, :, pl.ds(g * U, U)] = rp[s * 4 + g].astype(F32)
+                rpf[s, :, pl.ds(g * U, U)] = rp[s, g].astype(F32)
 
     def second_weights(n):
         return w2[:, :, pl.ds(n * C2, C2)].reshape(4 * U, C2)
@@ -326,8 +327,11 @@
         if t == 0:
             send_bias()
         if t == 1:
+            hand_refs()
+            hand_ref_parts()
+        if t == 2:
             make_feats()
-        if t == 2:
+        if t == 3:
             make_parts()
             done(w1_in, loc.at[0])
             done(w2_in, loc.at[1])
@@ -344,14 +348,16 @@
                     activate(i, EARLY)
             if 0 <= b < STEPS1 - 2 and i // 2 == b % 2:
                 multiply(b // 2, rows, LATE)
-        if b == STEPS1 - 2:
-            for i in range(4):
-                multiply(3, pl.ds(block_rows(i)[1], 256), LATE)
-                activate(i, LATE)
         n = t - L3 - STEPS1
         if n >= 0:
             theirs(n)
-            ours(n)
+        for i in range(4):
+            if b == STEPS1 - 2 + i // 2:
+                multiply(3, pl.ds(block_rows(i)[1], 256), LATE)
+                activate(i, LATE)
+        if n >= 1:
+            ours(n - 1)
+    ours(STEPS2 - 1)
     done(bs, small_recv.at[4])
     for n in range(STEPS2):
         finish_second(n)
@@ -361,7 +367,7 @@
     value = jnp.zeros((16, 128), F32)
     for j in range(2):
         place = z * 32 + mod(yy(4 - j), 2) * 16
-        total = jnp.sum(sacc[j], axis=1, keepdims=True)
+        total = jnp.sum(sacc[j], axis=1, keepdims=True) * (1.0 / 256.0)
         total = jnp.where(lane - place == jnp.bitwise_and(row, 15), total, 0.0)
         value += jnp.sum(total.reshape(16, 16, 128), axis=1)
     sm[...] = value
@@ -385,27 +391,21 @@
     done(bs.at[pl.ds(0, 7)], small_send.at[4])
     done(part_send, small_send.at[5])
 
-    def drain_refs():
-        done(rp.at[pl.ds(0, 7)], small_send.at[3])
-        done(feats.at[pl.ds(0, 112), pl.ds(0, 1024)], small_send.at[1])
-
-    def drain_others():
-        done(rp, small_send.at[3])
-        pl.when(x == z)(lambda: done(feats.at[pl.ds(0, 128), pl.ds(0, 1024)], small_send.at[1]))
-
-    pl.when(ref_self)(drain_refs)
-    pl.when(jnp.logical_not(ref_self))(drain_others)
+    done(ref.at[0], small_send.at[7])
+    done(rp.at[0], small_send.at[8])
+    pl.when(ref_self)(lambda: done(rp.at[0, pl.ds(0, 3)], small_send.at[3]))
+    pl.when(jnp.logical_not(ref_self))(lambda: done(rp.at[0], small_send.at[3]))
+    pl.when(ref_self)(lambda: done(feats.at[pl.ds(0, 48), pl.ds(0, 1024)], small_send.at[1]))
+    pl.when(jnp.logical_and(x == z, jnp.logical_not(ref_self)))(
+        lambda: done(feats.at[pl.ds(0, 64), pl.ds(0, 1024)], small_send.at[1])
+    )
 
     done(sc, small_recv.at[5])
     halves = [sc[4 * k] + sc[4 * k + 1] + sc[4 * k + 2] + sc[4 * k + 3] for k in range(2)]
     lane = lax.broadcasted_iota(jnp.int32, (16, 128), 1)
-    row = lax.broadcasted_iota(jnp.int32, (16, 128), 0)
     cross = jnp.bitwise_and(lane, 16) * (1 - y_hi) != 0
-    halves = [jnp.where(cross, halves[1 - k], halves[k]) for k in range(2)]
-    scores_out[:, pl.ds(0, 128)] = halves[0]
-    scores_out[:, pl.ds(128, 128)] = halves[1]
-    mean = jnp.sum(halves[0] + halves[1], axis=1, keepdims=True) * (1.0 / 256.0)
-    util_out[...] = jnp.sum(jnp.where(lane == row, mean, 0.0), axis=0, keepdims=True)[:, :16]
+    for k in range(2):
+        scores_out[:, pl.ds(k * 128, 128)] = jnp.where(cross, halves[1 - k], halves[k])
 
     pl.when(sc_self)(lambda: done(sc.at[pl.ds(0, 7)], small_send.at[6]))
     pl.when(jnp.logical_not(sc_self))(lambda: done(sc, small_send.at[6]))
@@ -415,18 +415,18 @@
     hbm = pl.BlockSpec(memory_space=pltpu.HBM)
     vmem = pl.BlockSpec(memory_space=pltpu.VMEM)
     dma = pltpu.SemaphoreType.DMA
-    scores, utilities = pl.pallas_call(
+    scores = pl.pallas_call(
         kernel,
-        out_shape=(jax.ShapeDtypeStruct((16, 256), F32), jax.ShapeDtypeStruct((1, 16), F32)),
+        out_shape=jax.ShapeDtypeStruct((16, 256), F32),
         in_specs=[hbm] * 8,
-        out_specs=(vmem, vmem),
+        out_specs=vmem,
         scratch_shapes=[
             pltpu.VMEM((2048, 4 * U), BF16),
             pltpu.VMEM((4, U, 1024), BF16),
             pltpu.VMEM((2, 16, 1024), BF16),
             pltpu.VMEM((2, 16, 1024), BF16),
             pltpu.VMEM((8, 16, U), BF16),
-            pltpu.VMEM((8, 16, U), BF16),
+            pltpu.VMEM((2, 4, 16, U), BF16),
             pltpu.VMEM((8, 2, 1, 128), F32),
             pltpu.VMEM((2, 1, 128), F32),
             pltpu.VMEM((1024, 2048), BF16),
@@ -442,7 +442,7 @@
             pltpu.VMEM((2, 16, 4 * U), F32),
             pltpu.VMEM((2, 256, 128), F32),
             dma((STEPS,)), dma((STEPS,)), dma((STEPS,)), dma((STEPS,)), dma((STEPS,)), dma((STEPS,)),
-            dma((2,)), dma((6,)), dma((7,)), dma((4,)), dma((2, STEPS2)),
+            dma((2,)), dma((8,)), dma((9,)), dma((4,)), dma((2, STEPS2)),
         ],
         compiler_params=pltpu.CompilerParams(
             collective_id=0, has_side_effects=True, vmem_limit_bytes=60 * 2**20
@@ -453,7 +453,7 @@
         hyp_emb, ref_emb, hyp_part, ref_part, pair_weight, out_weight.reshape(1, U, 1024),
         out_bias.reshape(1, 128), score_weight.reshape(1, 128),
     )
-    return scores, utilities.reshape(16)
+    return scores * 256.0, jnp.sum(scores, axis=1)
 
 
 def solution(mesh):

time: 64.5 us -> 60.2 us (0.933)
  Pallas kernels: 61.2 us -> 57.4 us
  local copies, waits for them, and re-layouts: 2.46 us -> 0 us
  other arithmetic: 0 us -> 1.95 us
    pallas_call x1, Pallas kernels: 61.2 us -> 57.4 us  [body(): pl.pallas_call(kernel, out_shape=jax.ShapeDtypeStruct((16, 256), F32), in...]
    unnamed x2 -> x0, local copies, waits for them, and re-layouts: 2.46 us -> none
    reduce_sum x0 -> x1, other arithmetic: none -> 1.95 us  [body(): return (scores * 256.0, jnp.sum(scores, axis=1))]
where the time goes in v3:
time: 60.2 us; the launch traced here: 60 us
  Pallas kernels  57.4 us (95%)
  other arithmetic  1.95 us (3%)
  between operations  0.64 us (1%)
    pallas_call x1, Pallas kernels, body(): pl.pallas_call(kernel, out_shape=jax.ShapeDtypeStruct((16, 256), F32), in...  57.4 us
    reduce_sum x1, other arithmetic, body(): return (scores * 256.0, jnp.sum(scores, axis=1))  1.95 us

profile of v3, /device:TPU:0, one launch (start us, length us, event | category | flops | bytes accessed | tf_op | source)
XLA Modules:
  0.0 60.0 jit_solution(17975780059384430466)
XLA Ops:
  0.6 57.4 %mbr_scores.1 = f32[16,256]{1,0:T(8,128)} custom-call(bf16[16,1024]{1,0:T(8,128)(2,1)} %hyp_emb.1, bf16[16,1024]{1,0:T(8,128)(2,1)} %ref_emb.1, bf16[16,384]{1,0:T(8,128)(2,1)} %hyp_part.1, bf16[16,384]{1,0:T(8,128)(2,1)} %ref_part.1, bf16[2048,384]{1,0:T(8,128)(2,1)} %w1_in.1, bf16[1,384,1024]{2,1,0:T(8,128)(2,1)} %bitcast.3, f32[1,128]{1,0:T(1,128)} %bitcast.4, ...), custom_call_target="tpu_custom_call" | custom-call | flops 9663676416 | bytes 3000000 | tf_op jit(solution)/shard_map/mbr_scores/pallas_call | solution.py:418
  58.1 1.9 %fusion = (f32[16]{0:T(128)}, f32[16,256]{1,0:T(8,128)}) fusion(f32[16,256]{1,0:T(8,128)} %mbr_scores.1), kind=kLoop, calls=%fused_computation.1 | loop fusion | flops 8176 | bytes 32832 | tf_op jit(solution)/shard_map/reduce_sum | solution.py:456

commit v4 on v3

v4 whole, which is shorter than its diff:
```python
import functools

import jax
import jax.numpy as jnp
from jax import lax
from jax.experimental import pallas as pl
from jax.experimental.pallas import tpu as pltpu
from jax.sharding import PartitionSpec as P

MESH = pl.DeviceIdType.MESH
BF16 = jnp.bfloat16
F32 = jnp.float32

STEPS1 = 8
STEPS2 = 4
STEPS = STEPS1 + STEPS2
K1 = 2048 // STEPS1
Q1 = K1 // 4
C2 = 1024 // STEPS2
U = 384
AHEAD = 3
EARLY = 3
LX, LD = 2, 3


def mod(a, n):
    return lax.rem(a, jnp.int32(n))


def half(a):
    return lax.div(a, jnp.int32(2))


def device(x, y, z, c):
    return ((half(y) * 4 + x) * 2 + c, mod(y, 2) * 4 + z)


def slot_of(rel):
    return rel + half(rel) * (5 - 2 * rel)


SLOT_AT = {0: 0, 1: 2, 2: 3, 3: 1}


def kernel(
    hyp_emb, ref_emb, hyp_part, ref_part, w1_in, w2_in, bias_in, score_in,
    scores_out,
    w1, w2, hyp, ref, hp, rp, bs, my_bs, feats, acc, first, part_send, part_recv, part_mine, sc, sm,
    hypf, reff, hpf, rpf, sacc,
    z_recv, z3_recv, y3_recv, x_recv, d_recv, w_send, small_recv, small_send, loc, pr_recv,
):
    blk = lax.axis_index("blk")
    hid = lax.axis_index("hid")
    c = mod(blk, 2)
    x = mod(half(blk), 4)
    y_hi = lax.div(blk, jnp.int32(8))
    y_lo = lax.div(hid, jnp.int32(4))
    y = y_hi * 2 + y_lo
    z = mod(hid, 4)

    def zz(d):
        return mod(z + d, 4)

    def yy(d):
        return mod(y + d, 4)

    def xx(d):
        return mod(x + d, 4)

    sibling = device(x, y, z, 1 - c)
    x_up, x_down = device(xx(1), y, z, c), device(xx(3), y, z, c)
    diagonal_up, diagonal_down = device(x, yy(1), zz(1), c), device(x, yy(3), zz(3), c)
    y_far, z_far = device(x, yy(2), z, c), device(x, y, zz(2), c)

    parity = mod(y_lo + z + c + x, 2)
    to_y, to_z = mod(2 * y_hi + c + parity, 4), x
    to_y2, to_z2 = mod(2 * y_hi + c, 4), xx(1)
    self_a = jnp.logical_and(to_y == y, to_z == z)
    self_b = jnp.logical_and(to_y2 == y, to_z2 == z)
    odd = parity == 1
    block_a = mod(c + y_lo, 2)
    has_b = c == y_lo

    barrier = pltpu.get_barrier_semaphore()

    def greet(target):
        pl.semaphore_signal(barrier, inc=1, device_id=target, device_id_type=MESH)

    for dy in range(4):
        for dz in range(4):
            if dy or dz:
                greet(device(x, yy(dy), zz(dz), c))
    greet(sibling)
    greet(x_up)
    greet(x_down)
    from_hi = half(mod(y + 4 - block_a, 4)) * 2
    for dz in range(4):
        source = device(z, from_hi + mod(y_lo + dz, 2), zz(dz), c)
        if dz == 0:
            pl.when(jnp.logical_not(jnp.logical_and(from_hi + y_lo == y, x == z)))(functools.partial(greet, source))
        else:
            greet(source)

    def greet_b():
        for dz in range(4):
            source = device(zz(3), y_hi * 2 + mod(y_lo + dz, 2), zz(dz), c)
            if dz == 0:
                pl.when(x != zz(3))(functools.partial(greet, source))
            else:
                greet(source)

    pl.when(has_b)(greet_b)
    expected = 15 + 3 + 4 - jnp.where(self_a, 1, 0) + jnp.where(odd, 4, 0) - jnp.where(jnp.logical_and(odd, self_b), 1, 0)
    pl.semaphore_wait(barrier, expected)

    def remote(src, dst, send, recv, target):
        pltpu.make_async_remote_copy(
            src_ref=src, dst_ref=dst, send_sem=send, recv_sem=recv, device_id=target, device_id_type=MESH
        ).start()

    def local(src, dst, sem):
        pltpu.make_async_copy(src, dst, sem).start()

    def done(region, sem):
        pltpu.make_async_copy(region, region, sem).wait()

    quarter = mod(x, 2) * 2 + c
    quarter_x = (1 - mod(x, 2)) * 2 + c

    def region(t, quarter_, slots, part=None):
        lo, n = slots
        size = Q1 if t < STEPS1 else 96
        first_row = quarter_ * size
        if part is not None:
            size //= 2
            first_row += part * size
        if t < STEPS1:
            rows = pl.ds(pl.multiple_of(t * K1 + first_row, size), size)
            return w1.at[rows, pl.ds(lo * U, n * U)]
        rows = pl.ds(pl.multiple_of(first_row, size), size)
        return w2.at[pl.ds(lo, n), rows, pl.ds((t - STEPS1) * C2, C2)]

    def own_piece(t, part=None):
        size = Q1 if t < STEPS1 else 96
        first_row = quarter * size
        if part is not None:
            size //= 2
            first_row += part * size
        if t < STEPS1:
            return w1_in.at[pl.ds(pl.multiple_of(t * K1 + first_row, size), size), :]
        rows = pl.ds(pl.multiple_of(first_row, size), size)
        return w2_in.at[:, rows, pl.ds((t - STEPS1) * C2, C2)]

    def send(src, dst, recv, target, t):
        remote(src, dst, w_send.at[0 if t < STEPS1 else 1], recv, target)

    def send_own(t):
        send(own_piece(t), region(t, quarter, (1, 1)), z_recv.at[t], diagonal_down, t)
        send(own_piece(t), region(t, quarter, (2, 1)), z_recv.at[t], diagonal_up, t)

    def send_own3(t):
        send(own_piece(t, y_hi), region(t, quarter, (3, 1), y_hi), z3_recv.at[t], z_far, t)

    local(hyp_emb, hyp.at[0], small_recv.at[0])
    remote(hyp_emb, hyp.at[1], small_send.at[0], small_recv.at[0], y_far)

    def send_four(src, there, send_sem, recv_sem, target_y, target_z, is_self):
        for k in range(4):
            target = device(xx(k), target_y, target_z, c)
            if k == 0:
                pl.when(is_self)(lambda: local(src, there, recv_sem))
                pl.when(jnp.logical_not(is_self))(lambda: remote(src, there, send_sem, recv_sem, target))
            else:
                remote(src, there, send_sem, recv_sem, target)

    for t in range(AHEAD):
        send_own3(t)
    for t in range(AHEAD):
        send_own(t)
    pl.when(x == z)(
        lambda: send_four(ref_emb, ref.at[parity], small_send.at[1], small_recv.at[1], to_y, to_z, self_a)
    )
    far_b = jnp.logical_and(odd, to_z2 == z)
    pl.when(far_b)(
        lambda: send_four(ref_emb, ref.at[2], small_send.at[10], small_recv.at[8], to_y2, to_z2, self_b)
    )
    local(w1_in, w1.at[:, pl.ds(0, U)], loc.at[0])
    local(w2_in, w2.at[pl.ds(0, 1)], loc.at[1])
    local(bias_in, my_bs.at[0], loc.at[2])
    local(score_in, my_bs.at[1], loc.at[3])
    local(hyp_part, hp.at[0], small_recv.at[2])
    for d in range(4):
        for flip in range(2):
            if d or flip:
                y_there = mod(y_hi + flip, 2) * 2 + mod(y_lo + d, 2)
                remote(
                    hyp_part, hp.at[flip * 4 + SLOT_AT[d]], small_send.at[2], small_recv.at[2],
                    device(x, y_there, zz(d), c),
                )
    slot_a, slot_b = slot_of(mod(z - x + 4, 4)), slot_of(mod(z - x + 3, 4))
    send_four(ref_part, rp.at[parity, slot_a], small_send.at[3], small_recv.at[3], to_y, to_z, self_a)
    pl.when(odd)(
        lambda: send_four(ref_part, rp.at[2, slot_b], small_send.at[9], small_recv.at[9], to_y2, to_z2, self_b)
    )

    def hand(block, direct, sem, other):
        done(block, direct)
        remote(block, block, sem, other, sibling)

    def hand_refs():
        hand(ref.at[block_a], small_recv.at[1], small_send.at[7], small_recv.at[6])
        pl.when(has_b)(lambda: hand(ref.at[2], small_recv.at[8], small_send.at[11], small_recv.at[8]))

    def hand_ref_parts():
        hand(rp.at[block_a], small_recv.at[3], small_send.at[8], small_recv.at[7])
        pl.when(has_b)(lambda: hand(rp.at[2], small_recv.at[9], small_send.at[12], small_recv.at[9]))

    def send_bias():
        done(bias_in, loc.at[2])
        done(score_in, loc.at[3])
        local(my_bs, bs.at[hid], small_recv.at[4])
        for d in range(1, 8):
            remote(my_bs, bs.at[hid], small_send.at[4], small_recv.at[4], (blk, mod(hid + d, 8)))

    def share(t):
        piece = region(t, quarter, (3, 1), y_hi)
        done(piece, z3_recv.at[t])
        send(piece, piece, y3_recv.at[t], y_far, t)
        if t + AHEAD < STEPS:
            send_own3(t + AHEAD)

    def forward_z(t):
        done(region(t, quarter, (1, 2)), z_recv.at[t])
        if t + AHEAD < STEPS:
            send_own(t + AHEAD)
        done(region(t, quarter, (3, 1), 1 - y_hi), y3_recv.at[t])
        for part, target in ((0, x_up), (1, x_down)):
            piece = region(t, quarter, (1, 3), part)
            send(piece, piece, x_recv.at[t], target, t)
        piece = region(t, quarter, (1, 3))
        send(piece, piece, d_recv.at[t], sibling, t)

    def forward_x(t):
        piece = region(t, quarter_x, (1, 3))
        done(piece, x_recv.at[t])
        send(piece, piece, d_recv.at[t], sibling, t)

    def arrived(t):
        if t < STEPS1:
            done(w1.at[pl.ds(0, 2 * Q1), pl.ds(0, 3 * U)], d_recv.at[t])
        else:
            done(w2.at[pl.ds(0, 3), pl.ds(0, 192), pl.ds(0, C2)], d_recv.at[t])

    FIRST_REF = (0, 16, 8, 40)

    def make_feats():
        done(hyp, small_recv.at[0])
        done(ref.at[1 - block_a], small_recv.at[6])
        pl.when(jnp.logical_not(has_b))(lambda: done(ref.at[2], small_recv.at[8]))
        hypf[...] = hyp[...].astype(F32)
        reff[...] = ref[...].astype(F32).reshape(48, 1024)

        def one(r, carry):
            for i in range(4):
                right = reff[pl.ds(FIRST_REF[i] + r, 1), :]
                for s in range(2):
                    left = hypf[s]
                    rows = pl.ds(pl.multiple_of(s * 512 + i * 128 + r * 16, 16), 16)
                    feats[rows, pl.ds(0, 1024)] = (left * right).astype(BF16)
                    feats[rows, pl.ds(1024, 1024)] = jnp.abs(left - right).astype(BF16)
            return carry

        lax.fori_loop(0, 8, one, 0)

    final = mod(y_lo + z, 2)
    mine = mod(y_hi + final, 2)

    K = 2 * K1

    def multiply(p, rows):
        left = feats[rows, pl.ds(p * K, K)]
        for n in range(3):
            columns = pl.ds(n * 512, 512)
            value = jnp.dot(left, w1[pl.ds(p * K, K), columns], preferred_element_type=F32)
            if p:
                value = acc[rows, columns] + value
            acc[rows, columns] = value

    def block_rows(i):
        slot = 1 - mine if i < 2 else mine
        return slot, pl.multiple_of(slot * 512 + (i % 2) * 256, 256)

    def activate(i):
        slot, base = block_rows(i)

        def one(r, carry):
            for j in range(2):
                here = pl.ds(pl.multiple_of(base + j * 128 + r * 16, 16), 16)
                there = pl.ds(pl.multiple_of(i * 256 + j * 128 + r * 16, 16), 16)
                row = FIRST_REF[2 * (i % 2) + j] + r
                value = acc[here, :] + hpf[slot] + rpf[pl.ds(row, 1), :]
                first[there, :] = jnp.tanh(value).astype(BF16)
            return carry

        lax.fori_loop(0, 8, one, 0)

    def make_parts():
        done(hp, small_recv.at[2])
        done(rp.at[1 - block_a], small_recv.at[7])
        pl.when(jnp.logical_not(has_b))(lambda: done(rp.at[2], small_recv.at[9]))
        for g in range(4):
            for s in range(2):
                hpf[s, :, pl.ds(g * U, U)] = hp[s * 4 + g].astype(F32)
            for k in range(3):
                rpf[pl.ds(k * 16, 16), pl.ds(g * U, U)] = rp[k, g].astype(F32)

    def second_weights(n):
        return w2[:, :, pl.ds(n * C2, C2)].reshape(4 * U, C2)

    def theirs(n, blocks=(0, 1)):
        columns = pl.ds(n * C2, C2)
        for j in blocks:
            rows = pl.ds(j * 256, 256)
            value = jnp.dot(first[rows, :], second_weights(n), preferred_element_type=F32)
            part_send[rows, columns] = value.astype(BF16)
            for i in (2 * j, 2 * j + 1):
                target = device(x, (yy(1), yy(3), y, y)[i], (z, z, zz(1), zz(3))[i], c)
                remote(
                    part_send.at[pl.ds(i * 128, 128), columns],
                    part_recv.at[pl.ds((i ^ 1) * 128, 128), columns],
                    small_send.at[5], pr_recv.at[n], target,
                )

    def ours(n):
        for j in range(2):
            rows = pl.ds(j * 256, 256)
            part_mine[rows, pl.ds(n * C2, C2)] = jnp.dot(
                first[pl.ds(512 + j * 256, 256), :], second_weights(n), preferred_element_type=F32
            )

    def finish_second(n):
        columns = pl.ds(n * C2, C2)
        done(part_recv.at[:, columns], pr_recv.at[n])
        for j in range(4):
            rows = pl.ds(j * 128, 128)
            total = jnp.zeros((128, 128), F32) if n == 0 else sacc[rows, :]
            for k in range(C2 // 128):
                g = n * (C2 // 128) + k
                lanes = pl.ds(g * 128, 128)
                value = part_mine[rows, lanes] + part_recv[rows, lanes].astype(F32)
                total += jnp.tanh(value + bs[g, 0]) * bs[g, 1]
            sacc[rows, :] = total

    for t in range(EARLY):
        share(t)
    for t in range(STEPS + LD):
        if t + EARLY < STEPS:
            share(t + EARLY)
        if t < STEPS:
            forward_z(t)
        if 0 <= t - LX < STEPS:
            forward_x(t - LX)
        if t == 0:
            send_bias()
            hand_refs()
            hand_ref_parts()
        if t == 1:
            make_feats()
        if t == 2:
            make_parts()
            done(w1_in, loc.at[0])
            done(w2_in, loc.at[1])
        if 0 <= t - LD < STEPS:
            arrived(t - LD)
        n = t - LD - STEPS1
        a = t - LD - 1
        for i in range(4):
            if 0 <= a < STEPS1 - 2 and i // 2 == a % 2:
                multiply(a // 2, pl.ds(block_rows(i)[1], 256))
            if a == STEPS1 - 2 + i and i < 2:
                multiply(3, pl.ds(block_rows(i)[1], 256))
                activate(i)
        if n == 0:
            theirs(0)
        if n >= 1:
            theirs(n)
            if n < 3:
                multiply(3, pl.ds(block_rows(n + 1)[1], 256))
                activate(n + 1)
    for n in range(STEPS2 - 1):
        ours(n)
    ours(STEPS2 - 1)
    done(bs, small_recv.at[4])
    for n in range(STEPS2):
        finish_second(n)

    lane = lax.broadcasted_iota(jnp.int32, (8, 16, 128), 2)
    row = lax.broadcasted_iota(jnp.int32, (8, 16, 128), 0)
    value = jnp.zeros((16, 128), F32)
    own_place = z * 32 + y_lo * 16
    places = (own_place, z * 32 + (1 - y_lo) * 16, own_place + 8, zz(3) * 32 + y_lo * 16 + 8)
    for i in range(4):
        total = jnp.sum(sacc[pl.ds(i * 128, 128), :].reshape(8, 16, 128), axis=2, keepdims=True) * (1.0 / 256.0)
        value += jnp.sum(jnp.where(lane - places[i] == row, total, 0.0), axis=0)
    sm[...] = value

    sc_row = y_hi * 4 + z
    sc_self = final == y_hi
    for d in range(8):
        target = (final * 8 + mod(blk, 8), mod(hid + d, 8))
        if d == 0:
            pl.when(sc_self)(lambda: local(sm, sc.at[sc_row], small_recv.at[5]))
            pl.when(jnp.logical_not(sc_self))(
                lambda: remote(sm, sc.at[sc_row], small_send.at[6], small_recv.at[5], target)
            )
        else:
            remote(sm, sc.at[sc_row], small_send.at[6], small_recv.at[5], target)

    done(w1.at[pl.ds(0, 3 * 512), :], w_send.at[0])
    done(w2.at[pl.ds(0, 3)], w_send.at[1])
    done(hyp.at[0], small_send.at[0])
    done(hp.at[pl.ds(0, 7)], small_send.at[2])
    done(bs.at[pl.ds(0, 7)], small_send.at[4])
    done(part_send, small_send.at[5])

    done(ref.at[0], small_send.at[7])
    done(rp.at[0], small_send.at[8])

    def drain_b():
        done(ref.at[0], small_send.at[11])
        done(rp.at[0], small_send.at[12])

    pl.when(has_b)(drain_b)

    def drain_four(three, four, sem, is_self):
        pl.when(is_self)(lambda: done(three, sem))
        pl.when(jnp.logical_not(is_self))(lambda: done(four, sem))

    three_embs, four_embs = ref, feats.at[pl.ds(0, 64), pl.ds(0, 1024)]
    three_parts, four_parts = rp.at[0, pl.ds(0, 3)], rp.at[0]
    drain_four(three_parts, four_parts, small_send.at[3], self_a)
    pl.when(odd)(lambda: drain_four(three_parts, four_parts, small_send.at[9], self_b))
    pl.when(x == z)(lambda: drain_four(three_embs, four_embs, small_send.at[1], self_a))
    pl.when(far_b)(lambda: drain_four(three_embs, four_embs, small_send.at[10], self_b))

    done(sc, small_recv.at[5])
    lane = lax.broadcasted_iota(jnp.int32, (16, 128), 1)
    halves = [jnp.zeros((16, 128), F32), jnp.zeros((16, 128), F32)]
    for k in range(4):
        cross = jnp.bitwise_and(lane, 16) * (1 - mod(y_hi + k, 2)) != 0
        low, high = sc[k], sc[4 + k]
        halves[0] += jnp.where(cross, high, low)
        halves[1] += jnp.where(cross, low, high)
    for k in range(2):
        scores_out[:, pl.ds(k * 128, 128)] = halves[k]

    pl.when(sc_self)(lambda: done(sc.at[pl.ds(0, 7)], small_send.at[6]))
    pl.when(jnp.logical_not(sc_self))(lambda: done(sc, small_send.at[6]))


def body(hyp_emb, ref_emb, hyp_part, ref_part, pair_weight, out_weight, out_bias, score_weight):
    hbm = pl.BlockSpec(memory_space=pltpu.HBM)
    vmem = pl.BlockSpec(memory_space=pltpu.VMEM)
    dma = pltpu.SemaphoreType.DMA
    scores = pl.pallas_call(
        kernel,
        out_shape=jax.ShapeDtypeStruct((16, 256), F32),
        in_specs=[hbm] * 8,
        out_specs=vmem,
        scratch_shapes=[
            pltpu.VMEM((2048, 4 * U), BF16),
            pltpu.VMEM((4, U, 1024), BF16),
            pltpu.VMEM((2, 16, 1024), BF16),
            pltpu.VMEM((3, 16, 1024), BF16),
            pltpu.VMEM((8, 16, U), BF16),
            pltpu.VMEM((3, 4, 16, U), BF16),
            pltpu.VMEM((8, 2, 1, 128), F32),
            pltpu.VMEM((2, 1, 128), F32),
            pltpu.VMEM((1024, 2048), BF16),
            pltpu.VMEM((1024, 4 * U), F32),
            pltpu.VMEM((1024, 4 * U), BF16),
            pltpu.VMEM((512, 1024), BF16),
            pltpu.VMEM((512, 1024), BF16),
            pltpu.VMEM((512, 1024), F32),
            pltpu.VMEM((8, 16, 128), F32),
            pltpu.VMEM((16, 128), F32),
            pltpu.VMEM((2, 16, 1024), F32),
            pltpu.VMEM((48, 1024), F32),
            pltpu.VMEM((2, 16, 4 * U), F32),
            pltpu.VMEM((48, 4 * U), F32),
            pltpu.VMEM((512, 128), F32),
            dma((STEPS,)), dma((STEPS,)), dma((STEPS,)), dma((STEPS,)), dma((STEPS,)),
            dma((2,)), dma((10,)), dma((13,)), dma((4,)), dma((STEPS2,)),
        ],
        compiler_params=pltpu.CompilerParams(
            collective_id=0, has_side_effects=True, vmem_limit_bytes=60 * 2**20
        ),
        cost_estimate=pl.CostEstimate(flops=9_663_676_416, bytes_accessed=3_000_000, transcendentals=2_097_152),
        name="mbr_scores",
    )(
        hyp_emb, ref_emb, hyp_part, ref_part, pair_weight, out_weight.reshape(1, U, 1024),
        out_bias.reshape(1, 128), score_weight.reshape(1, 128),
    )
    return scores * 256.0, jnp.sum(scores, axis=1)


def solution(mesh):
    in_specs = (
        P("blk", None),
        P("blk", None),
        P("blk", "hid"),
        P("blk", "hid"),
        P(None, "hid"),
        P("hid", None),
        P("hid"),
        P("hid"),
    )
    out_specs = (P("blk", None), P("blk"))
    return jax.shard_map(body, mesh=mesh, in_specs=in_specs, out_specs=out_specs, check_vma=False)
```

time: 60.2 us -> 58.5 us (0.972)
  Pallas kernels: 57.4 us -> 55.8 us
    pallas_call x1, Pallas kernels: 57.4 us -> 55.8 us  [body(): pl.pallas_call(kernel, out_shape=jax.ShapeDtypeStruct((16, 256), F32), in...]
where the time goes in v4:
time: 58.5 us; the launch traced here: 58.3 us
  Pallas kernels  55.8 us (95%)
  other arithmetic  1.95 us (3%)
  between operations  0.64 us (1%)
    pallas_call x1, Pallas kernels, body(): pl.pallas_call(kernel, out_shape=jax.ShapeDtypeStruct((16, 256), F32), in...  55.8 us
    reduce_sum x1, other arithmetic, body(): return (scores * 256.0, jnp.sum(scores, axis=1))  1.95 us

profile of v4, /device:TPU:0, one launch (start us, length us, event | category | flops | bytes accessed | tf_op | source)
XLA Modules:
  0.0 58.3 jit_solution(13481589278262180013)
XLA Ops:
  0.6 55.8 %mbr_scores.1 = f32[16,256]{1,0:T(8,128)} custom-call(bf16[16,1024]{1,0:T(8,128)(2,1)} %hyp_emb.1, bf16[16,1024]{1,0:T(8,128)(2,1)} %ref_emb.1, bf16[16,384]{1,0:T(8,128)(2,1)} %hyp_part.1, bf16[16,384]{1,0:T(8,128)(2,1)} %ref_part.1, bf16[2048,384]{1,0:T(8,128)(2,1)} %w1_in.1, bf16[1,384,1024]{2,1,0:T(8,128)(2,1)} %bitcast.3, f32[1,128]{1,0:T(1,128)} %bitcast.4, ...), custom_call_target="tpu_custom_call" | custom-call | flops 9663676416 | bytes 3000000 | tf_op jit(solution)/shard_map/mbr_scores/pallas_call | solution.py:465
  56.4 1.9 %fusion = (f32[16]{0:T(128)}, f32[16,256]{1,0:T(8,128)}) fusion(f32[16,256]{1,0:T(8,128)} %mbr_scores.1), kind=kLoop, calls=%fused_computation.1 | loop fusion | flops 8176 | bytes 32832 | tf_op jit(solution)/shard_map/reduce_sum | solution.py:504

commit v5 on v4

--- a/solution.py
+++ b/solution.py
@@ -279,12 +279,10 @@
 
     def multiply(p, rows):
         left = feats[rows, pl.ds(p * K, K)]
-        for n in range(3):
-            columns = pl.ds(n * 512, 512)
-            value = jnp.dot(left, w1[pl.ds(p * K, K), columns], preferred_element_type=F32)
-            if p:
-                value = acc[rows, columns] + value
-            acc[rows, columns] = value
+        value = jnp.dot(left, w1[pl.ds(p * K, K), :], preferred_element_type=F32)
+        if p:
+            value = acc[rows, :] + value
+        acc[rows, :] = value
 
     def block_rows(i):
         slot = 1 - mine if i < 2 else mine
@@ -374,6 +372,8 @@
             arrived(t - LD)
         n = t - LD - STEPS1
         a = t - LD - 1
+        if n == 0:
+            theirs(0, (0,))
         for i in range(4):
             if 0 <= a < STEPS1 - 2 and i // 2 == a % 2:
                 multiply(a // 2, pl.ds(block_rows(i)[1], 256))
@@ -381,7 +381,7 @@
                 multiply(3, pl.ds(block_rows(i)[1], 256))
                 activate(i)
         if n == 0:
-            theirs(0)
+            theirs(0, (1,))
         if n >= 1:
             theirs(n)
             if n < 3:

time: 58.5 us -> 58.8 us (level)
  no operation moved by 1% of the time
where the time goes in v5:
time: 58.8 us; the launch traced here: 58.6 us
  Pallas kernels  56 us (95%)
  other arithmetic  1.95 us (3%)
  between operations  0.64 us (1%)
    pallas_call x1, Pallas kernels, body(): pl.pallas_call(kernel, out_shape=jax.ShapeDtypeStruct((16, 256), F32), in...  56 us
    reduce_sum x1, other arithmetic, body(): return (scores * 256.0, jnp.sum(scores, axis=1))  1.95 us

profile of v5, /device:TPU:0, one launch (start us, length us, event | category | flops | bytes accessed | tf_op | source)
XLA Modules:
  0.0 58.6 jit_solution(17313275067686544220)
XLA Ops:
  0.6 56.0 %mbr_scores.1 = f32[16,256]{1,0:T(8,128)} custom-call(bf16[16,1024]{1,0:T(8,128)(2,1)} %hyp_emb.1, bf16[16,1024]{1,0:T(8,128)(2,1)} %ref_emb.1, bf16[16,384]{1,0:T(8,128)(2,1)} %hyp_part.1, bf16[16,384]{1,0:T(8,128)(2,1)} %ref_part.1, bf16[2048,384]{1,0:T(8,128)(2,1)} %w1_in.1, bf16[1,384,1024]{2,1,0:T(8,128)(2,1)} %bitcast.3, f32[1,128]{1,0:T(1,128)} %bitcast.4, ...), custom_call_target="tpu_custom_call" | custom-call | flops 9663676416 | bytes 3000000 | tf_op jit(solution)/shard_map/mbr_scores/pallas_call | solution.py:465
  56.6 1.9 %fusion = (f32[16]{0:T(128)}, f32[16,256]{1,0:T(8,128)}) fusion(f32[16,256]{1,0:T(8,128)} %mbr_scores.1), kind=kLoop, calls=%fused_computation.1 | loop fusion | flops 8176 | bytes 32832 | tf_op jit(solution)/shard_map/reduce_sum | solution.py:504
